TPU v7x, 512 devices: a whole 4x4x16 slice. The times are simulated.
512 devices in a mesh: row: 32 (over x, y, core), col: 16 (over z).
Axes of the slice: x: 4, y: 4, z: 16, core: 2. Of those that a mesh axis runs over, the one named last changes fastest.
Arguments:
- points: float32 [128, 65536], P(None, ('row', 'col')), may hold values from -6 to 6
- solution: float32 [16, 65536], P(None, ('row', 'col')), may hold values from -6 to 6
- residual: float32 [16, 65536], P(None, ('row', 'col')), may hold values from -23 to 23, as said below
- direction: float32 [16, 65536], P(None, ('row', 'col')), may hold values from -23 to 23, as said below
Outputs:
- next_solution: float32 [16, 65536], P(None, ('row', 'col'))
- next_residual: float32 [16, 65536], P(None, ('row', 'col'))
- next_direction: float32 [16, 65536], P(None, ('row', 'col'))
Inputs may be any that keep to these rules, and one draw needn't show every extreme that they name: `residual`: Real-valued entries. `direction`: Real-valued entries.
All inputs are finite; a program needn't handle non-finite values.
Results may differ from a plain program's by a relative error of at most 0.00024.
Values sent between devices are 32-bit elements; how exact they have to be, the bound alone decides.
A program may use at most 64 MiB of HBM per device.

v0:
```python
import math

import jax
import jax.numpy as jnp
from jax import lax
from jax.sharding import PartitionSpec as P

noise_var = 0.5
inv_two_len = 0.03125


def kernel_product(carry_sum, pts_piece, dir_piece, rows_pts, rows_sq):
    products = lax.dot_general(
        pts_piece,
        rows_pts,
        (((0,), (0,)), ((), ())),
        precision=lax.Precision.HIGHEST,
        preferred_element_type=jnp.float32,
    )
    piece_sq = jnp.sum(pts_piece * pts_piece, axis=0)
    distance = piece_sq[:, None] + rows_sq[None, :] - 2.0 * products
    kernel_tile = jnp.exp(-inv_two_len * distance)
    return carry_sum + jnp.dot(
        dir_piece, kernel_tile, precision=lax.Precision.HIGHEST, preferred_element_type=jnp.float32
    )


def fold_columns(rows_pts, rows_sq, carry_sum, pieces):
    pts_piece, dir_piece = pieces
    span_cols = pts_piece.shape[1]
    block_cols = math.gcd(span_cols, 512)
    block_count = span_cols // block_cols

    def scan_step(running, block_index):
        offset = block_index * block_cols
        pts_block = lax.dynamic_slice_in_dim(pts_piece, offset, block_cols, 1)
        dir_block = lax.dynamic_slice_in_dim(dir_piece, offset, block_cols, 1)
        return (kernel_product(running, pts_block, dir_block, rows_pts, rows_sq), None)

    result_sum, _ = lax.scan(scan_step, carry_sum, jnp.arange(block_count, dtype=jnp.int32))
    return result_sum


def residual_norm(next_residual):
    return lax.psum(jnp.sum(next_residual * next_residual, axis=1), ("row", "col"))


def per_device(points, solution, residual, direction):
    rows_pts = lax.all_gather(points, "col", axis=1, tiled=True)
    rows_sq = jnp.sum(rows_pts * rows_pts, axis=0)
    initial = jnp.zeros((direction.shape[0], rows_pts.shape[1]), jnp.float32)
    partial_value = fold_columns(
        rows_pts,
        rows_sq,
        initial,
        (
            lax.all_gather(points, "row", axis=1, tiled=True),
            lax.all_gather(direction, "row", axis=1, tiled=True),
        ),
    )
    applied = lax.psum_scatter(partial_value, "col", scatter_dimension=1, tiled=True)
    applied = applied + noise_var * direction
    norm_now, curvature = lax.psum(
        (jnp.sum(residual * residual, axis=1), jnp.sum(direction * applied, axis=1)), ("row", "col")
    )
    step_size = norm_now / curvature
    next_solution = solution + step_size[:, None] * direction
    next_residual = residual - step_size[:, None] * applied
    norm_next = residual_norm(next_residual)
    ratio = norm_next / norm_now
    next_direction = next_residual + ratio[:, None] * direction
    return (next_solution, next_residual, next_direction)


def solution(mesh):
    return jax.shard_map(
        per_device,
        mesh=mesh,
        in_specs=(
            P(None, ("row", "col")),
            P(None, ("row", "col")),
            P(None, ("row", "col")),
            P(None, ("row", "col")),
        ),
        out_specs=(P(None, ("row", "col")), P(None, ("row", "col")), P(None, ("row", "col"))),
        check_vma=False,
    )
```

profile of v0, /device:TPU:1, one launch (start us, length us, event | category | flops | bytes accessed | tf_op | source)
XLA Modules:
  0.0 538.6 jit_solution(16004049946409653586)
XLA Ops:
  8.7 27.6 %all_gather.9 = f32[16,4096]{1,0:T(8,128)S(1)} all-gather(f32[16,128]{1,0:T(8,128)} %param.9), channel_id=1, replica_groups=mesh['row'=32,'col'=16] {'row'}, dimensions={1}, use_global_device_ids=true | all-gather | bytes 270336 | tf_op jit(solution)/shard_map/all_gather | solution.py:58
  36.3 40.4 %all-gather.5.cloned.1.call-done = f32[128,2048]{1,0:T(8,128)} async-done(((f32[128,128]{1,0:T(8,128)}), f32[128,2048]{1,0:T(8,128)}) %all-gather.5.cloned.1.call-update) | async-done | bytes 1048592 | tf_op jit(solution)/shard_map/all_gather | solution.py:49
  76.7 1.3 multiply_reduce_fusion.1
  78.0 69.0 %all-gather.3.cloned.1.call-done = f32[128,4096]{1,0:T(8,128)} async-done(((f32[128,128]{1,0:T(8,128)}), f32[128,4096]{1,0:T(8,128)}) %all-gather.3.cloned.1.call-update) | async-done | bytes 2097168 | tf_op jit(solution)/shard_map/all_gather | solution.py:57
  147.0 112.3 %while.11 = (s32[]{:T(128)}, f32[16,2048]{1,0:T(8,128)S(1)}, s32[8]{0:T(128)S(1)}, f32[16,4096]{1,0:T(8,128)S(1)}, f32[128,4096]{1,0:T(8,128)}, /*index=5*/f32[2...) while((s32[]{:T(128)}, f32[16,2048]{1,0:T(8,128)S(1)}, ...), condition=%wide.region_5.6_spmd.clone, body=%wide.region_3.0_spmd.clone.sunk | while | flops 1816329728 | bytes 10268861 | solution.py:40
  148.3 6.7 %fusion.31 = f32[512,2048]{1,0:T(8,128)} fusion(f32[128,2048]{1,0:T(8,128)} %get-tuple-element.155, f32[128,4096]{1,0:T(8,128)} %get-tuple-element.153, s32[]{:T(128)S(6)} %select_n.6), kind=kOutput, calls=%fused_computation.12.clone.1 | convolution fusion | flops 1610612736 | bytes 5505028 | tf_op jit(solution)/shard_map/while/body/eval_jaxpr/dot_general | solution.py:13
  155.0 1.0 multiply_reduce_fusion.6
  156.0 5.1 fusion.32
  162.3 6.7 %fusion.31 = f32[512,2048]{1,0:T(8,128)} fusion(f32[128,2048]{1,0:T(8,128)} %get-tuple-element.155, f32[128,4096]{1,0:T(8,128)} %get-tuple-element.153, s32[]{:T(128)S(6)} %select_n.6), kind=kOutput, calls=%fused_computation.12.clone.1 | convolution fusion | flops 1610612736 | bytes 5505028 | tf_op jit(solution)/shard_map/while/body/eval_jaxpr/dot_general | solution.py:13
  169.0 1.0 multiply_reduce_fusion.6
  170.0 5.1 fusion.32
  176.4 6.7 %fusion.31 = f32[512,2048]{1,0:T(8,128)} fusion(f32[128,2048]{1,0:T(8,128)} %get-tuple-element.155, f32[128,4096]{1,0:T(8,128)} %get-tuple-element.153, s32[]{:T(128)S(6)} %select_n.6), kind=kOutput, calls=%fused_computation.12.clone.1 | convolution fusion | flops 1610612736 | bytes 5505028 | tf_op jit(solution)/shard_map/while/body/eval_jaxpr/dot_general | solution.py:13
  183.1 1.0 multiply_reduce_fusion.6
  184.1 5.1 fusion.32
  190.4 6.7 %fusion.31 = f32[512,2048]{1,0:T(8,128)} fusion(f32[128,2048]{1,0:T(8,128)} %get-tuple-element.155, f32[128,4096]{1,0:T(8,128)} %get-tuple-element.153, s32[]{:T(128)S(6)} %select_n.6), kind=kOutput, calls=%fused_computation.12.clone.1 | convolution fusion | flops 1610612736 | bytes 5505028 | tf_op jit(solution)/shard_map/while/body/eval_jaxpr/dot_general | solution.py:13
  197.1 1.0 multiply_reduce_fusion.6
  198.1 5.1 fusion.32
  204.4 6.7 %fusion.31 = f32[512,2048]{1,0:T(8,128)} fusion(f32[128,2048]{1,0:T(8,128)} %get-tuple-element.155, f32[128,4096]{1,0:T(8,128)} %get-tuple-element.153, s32[]{:T(128)S(6)} %select_n.6), kind=kOutput, calls=%fused_computation.12.clone.1 | convolution fusion | flops 1610612736 | bytes 5505028 | tf_op jit(solution)/shard_map/while/body/eval_jaxpr/dot_general | solution.py:13
  211.1 1.0 multiply_reduce_fusion.6
  212.1 5.1 fusion.32
  218.5 6.7 %fusion.31 = f32[512,2048]{1,0:T(8,128)} fusion(f32[128,2048]{1,0:T(8,128)} %get-tuple-element.155, f32[128,4096]{1,0:T(8,128)} %get-tuple-element.153, s32[]{:T(128)S(6)} %select_n.6), kind=kOutput, calls=%fused_computation.12.clone.1 | convolution fusion | flops 1610612736 | bytes 5505028 | tf_op jit(solution)/shard_map/while/body/eval_jaxpr/dot_general | solution.py:13
  225.2 1.0 multiply_reduce_fusion.6
  226.2 5.1 fusion.32
  232.5 6.7 %fusion.31 = f32[512,2048]{1,0:T(8,128)} fusion(f32[128,2048]{1,0:T(8,128)} %get-tuple-element.155, f32[128,4096]{1,0:T(8,128)} %get-tuple-element.153, s32[]{:T(128)S(6)} %select_n.6), kind=kOutput, calls=%fused_computation.12.clone.1 | convolution fusion | flops 1610612736 | bytes 5505028 | tf_op jit(solution)/shard_map/while/body/eval_jaxpr/dot_general | solution.py:13
  239.2 1.0 multiply_reduce_fusion.6
  240.2 5.1 fusion.32
  246.6 6.7 %fusion.31 = f32[512,2048]{1,0:T(8,128)} fusion(f32[128,2048]{1,0:T(8,128)} %get-tuple-element.155, f32[128,4096]{1,0:T(8,128)} %get-tuple-element.153, s32[]{:T(128)S(6)} %select_n.6), kind=kOutput, calls=%fused_computation.12.clone.1 | convolution fusion | flops 1610612736 | bytes 5505028 | tf_op jit(solution)/shard_map/while/body/eval_jaxpr/dot_general | solution.py:13
  254.2 5.1 fusion.32
  260.1 56.3 %reduce-scatter.2.cloned.1.call-done = f32[16,128]{1,0:T(8,128)} async-done(((f32[16,2048]{1,0:T(8,128)}), f32[16,128]{1,0:T(8,128)}) %reduce-scatter.2.cloned.1.call-update) | async-done | bytes 8208 | tf_op jit(solution)/shard_map/reduce_scatter | solution.py:61
  317.2 112.5 %all-reduce = (f32[16]{0:T(128)S(1)}, f32[16]{0:T(128)S(1)}) all-reduce(f32[16]{0:T(128)S(1)} %multiply_reduce_fusion.4, f32[16]{0:T(128)S(1)} %multiply_reduce_fusion.3), channel_id=1, replica_groups=mesh['row'=32,'col'=16] {'row','col'}, use_global_device_ids=true, to_apply=%region_1.2 | all-reduce | flops 32 | bytes 256 | tf_op jit(solution)/shard_map/psum | solution.py:63
  429.7 1.5 multiply_reduce_fusion.2
  431.2 100.1 %psum.23 = f32[16]{0:T(128)S(1)} all-reduce(f32[16]{0:T(128)S(1)} %get-tuple-element.81), channel_id=1, replica_groups=mesh['row'=32,'col'=16] {'row','col'}, use_global_device_ids=true, to_apply=%region_10.11 | all-reduce | flops 16 | bytes 128 | tf_op jit(solution)/shard_map/psum | solution.py:45
  (32 shorter events, 9.5 us)
Async XLA Ops:
  7.2 69.5 %all-gather.5.cloned.1.call-start = ((), (), s32[]{:S(2)}) async-start(), calls=%async_computation.2 | async-start | bytes 1114112 | tf_op jit(solution)/shard_map/all_gather | solution.py:49
  7.9 139.1 %all-gather.3.cloned.1.call-start = ((), (), s32[]{:S(2)}) async-start(), calls=%async_computation.1 | async-start | bytes 2162688 | tf_op jit(solution)/shard_map/all_gather | solution.py:57
  8.6 307.8 %reduce-scatter.2.cloned.1.call-start = ((), (), s32[]{:S(2)}) async-start(), calls=%async_computation.3 | async-start | bytes 139264 | tf_op jit(solution)/shard_map/reduce_scatter | solution.py:61
  147.0 113.0 %copy-start.3 = (f32[16,128]{1,0:T(8,128)S(1)}, f32[16,128]{1,0:T(8,128)}, u32[]{:S(2)}) copy-start(f32[16,128]{1,0:T(8,128)} %param.8) | copy-start | bytes 24580
  147.0 169.4 %copy-start = (f32[16,128]{1,0:T(8,128)S(1)}, f32[16,128]{1,0:T(8,128)}, u32[]{:S(2)}) copy-start(f32[16,128]{1,0:T(8,128)} %param.9) | copy-start | bytes 24580
  147.0 282.7 %copy-start.4 = (f32[16,128]{1,0:T(8,128)S(1)}, f32[16,128]{1,0:T(8,128)}, u32[]{:S(2)}) copy-start(f32[16,128]{1,0:T(8,128)} %param.7) | copy-start | bytes 24580
  259.3 0.6 copy-start.1
  431.2 100.8 %copy-start.2 = (f32[16,128]{1,0:T(8,128)}, f32[16,128]{1,0:T(8,128)S(1)}, u32[]{:S(2)}) copy-start(f32[16,128]{1,0:T(8,128)S(1)} %get-tuple-element.82) | copy-start | bytes 24580
Sparse Core Ops, SparseCore 0:
  10.0 66.6 all-gather.4
  79.8 67.2 all-gather.2
  260.1 56.2 reduce-scatter.1
where the time goes:
time: 540 us; the launch traced here: 539 us
  blocking collectives  240 us (44%)
  waiting for transfers between devices  167 us (31%)
  matrix products  94.4 us (17%)
  between operations  13.8 us (3%)
  other arithmetic  12.3 us (2%)
    psum x1, blocking collectives, per_device(): lax.psum((jnp.sum(residual * residual, axis=1), jnp.sum(direction * appli...  112 us
    psum x1, blocking collectives, residual_norm(): lax.psum(jnp.sum(next_residual * next_residual, axis=1), ('row', 'col'))  100 us
    all_gather x1, waiting for transfers between devices, per_device(): lax.all_gather(points, 'row', axis=1, tiled=True)  69 us
    reduce_scatter x1, waiting for transfers between devices, per_device(): lax.psum_scatter(partial_value, 'col', scatter_dimension=1, tiled=True)  56.3 us
    dot_general x8, matrix products, kernel_product(): lax.dot_general(pts_piece, rows_pts, (((0,), (0,)), ((), ())), precision=...  53.7 us
    dot_general x8, matrix products, kernel_product(): jnp.dot(dir_piece, kernel_tile, precision=lax.Precision.HIGHEST, preferre...  40.7 us
    all_gather x1, waiting for transfers between devices, per_device(): rows_pts = lax.all_gather(points, 'col', axis=1, tiled=True)  40.4 us
    all_gather x1, blocking collectives, per_device(): lax.all_gather(direction, 'row', axis=1, tiled=True)  27.6 us
  transfers between devices with their start and end apart: 3, of which 3 were waited for; matrix products, arithmetic and copies ran while one was open for 0% of the time, Pallas kernels for 0%

commit v1 on v0

v1 whole, which is shorter than its diff:
```python
import functools
import math

import jax
import jax.numpy as jnp
from jax import lax
from jax.experimental import pallas as pl
from jax.experimental.pallas import tpu as pltpu
from jax.sharding import PartitionSpec as P

noise_var = 0.5
inv_two_len = 0.03125
scale = inv_two_len * math.log2(math.e)

MESH = pl.DeviceIdType.MESH
f32 = jnp.float32
bf16 = jnp.bfloat16

side = 4
rows_n = 32
cols_n = 16
block = 128
rhs = 16
chunk = 1024
pairs = 8

offsets = sorted(
    [(dx, dy) for dx in range(side) for dy in range(side)],
    key=lambda d: (min(d[0], side - d[0]) + min(d[1], side - d[1]), max(min(d[0], side - d[0]), min(d[1], side - d[1]))),
)
plane = len(offsets)


def split(values):
    high = values.astype(bf16)
    low = (values - high.astype(f32)).astype(bf16)
    return high, low


def kernel(
    pts_ref,
    sol_ref,
    res_ref,
    dir_ref,
    nsol_ref,
    nres_ref,
    ndir_ref,
    col_in,
    row_in,
    weights,
    row_sq,
    stream,
    col_sq,
    dirs,
    tile_a,
    tile_b,
    total,
    part,
    part_in,
    stat_z,
    stat_r,
    col_send,
    col_recv,
    sib_send,
    sib_recv,
    row_send,
    row_recv,
    part_send,
    part_recv,
    sz_send,
    sz_recv,
    sr_send,
    sr_recv,
):
    r = lax.axis_index("row")
    z = lax.axis_index("col")
    x, y, core = r // 8, (r // 2) % 4, r % 2
    sibling = r + 1 - 2 * core
    up, down = (z + 1) % cols_n, (z + cols_n - 1) % cols_n

    barrier = pltpu.get_barrier_semaphore()

    @pl.loop(1, cols_n)
    def _(step):
        pl.semaphore_signal(barrier, inc=1, device_id=(r, (z + step) % cols_n), device_id_type=MESH)

    @pl.loop(1, rows_n)
    def _(step):
        pl.semaphore_signal(barrier, inc=1, device_id=((r + step) % rows_n, z), device_id_type=MESH)

    row_in[0] = pts_ref[...]
    col_in[0, 0, 0:block, :] = pts_ref[...].T
    col_in[0, 0, block : block + rhs, :] = dir_ref[...]
    total[...] = jnp.zeros_like(total)

    pl.semaphore_wait(barrier, cols_n - 1 + rows_n - 1)

    def row_copy(src, dst, target):
        return pltpu.make_async_remote_copy(
            src_ref=row_in.at[src],
            dst_ref=row_in.at[dst],
            send_sem=row_send.at[dst],
            recv_sem=row_recv.at[dst],
            device_id=(r, target),
            device_id_type=MESH,
        )

    def col_copy(o):
        dx, dy = offsets[o]
        target = (((x + side - dx) % side) * side + (y + side - dy) % side) * 2 + core
        return pltpu.make_async_remote_copy(
            src_ref=col_in.at[0, 0],
            dst_ref=col_in.at[0, o],
            send_sem=col_send.at[o],
            recv_sem=col_recv.at[o],
            device_id=(target, z),
            device_id_type=MESH,
        )

    def sib_copy(o):
        return pltpu.make_async_remote_copy(
            src_ref=col_in.at[0, o],
            dst_ref=col_in.at[1, o],
            send_sem=sib_send.at[o],
            recv_sem=sib_recv.at[o],
            device_id=(sibling, z),
            device_id_type=MESH,
        )

    def part_copy(slot, dst, target):
        return pltpu.make_async_remote_copy(
            src_ref=part.at[slot],
            dst_ref=part_in.at[dst],
            send_sem=part_send.at[slot],
            recv_sem=part_recv.at[dst],
            device_id=(r, target),
            device_id_type=MESH,
        )

    row_copy(0, 1, down).start()
    row_copy(0, 2, up).start()
    sib_copy(0).start()
    for o in range(1, plane):
        col_copy(o).start()

    def make_weights(p, half, slot):
        pts = row_in[slot]
        high, low = split(pts * (2.0 * scale))
        lanes = slice(half * block, (half + 1) * block)
        weights[p, 0 * block : 1 * block, lanes] = high
        weights[p, 1 * block : 2 * block, lanes] = low
        weights[p, 2 * block : 3 * block, lanes] = high
        weights[p, 3 * block : 4 * block, lanes] = low
        row_sq[p, :, lanes] = jnp.broadcast_to(scale * jnp.sum(pts * pts, axis=0, keepdims=True), (8, block))

    def make_stream(b, o):
        place = pl.ds(pl.multiple_of((2 * o + b) * block, block), block)
        pts = col_in[b, o, 0:block, :]
        high, low = split(pts)
        stream[place, 0 * block : 1 * block] = high
        stream[place, 1 * block : 2 * block] = high
        stream[place, 2 * block : 3 * block] = low
        stream[place, 3 * block : 4 * block] = low
        col_sq[place, :] = jnp.broadcast_to(scale * jnp.sum(pts * pts, axis=1, keepdims=True), (block, block))
        high, low = split(col_in[b, o, block : block + rhs, :])
        dirs[0:rhs, place] = high
        dirs[rhs : 2 * rhs, place] = low

    def take_columns(c):
        for i in range(4):
            o = 4 * c + i
            if o > 0:
                col_copy(o).wait_recv()
                sib_copy(o).start()
            make_stream(0, o)
        for i in range(4):
            o = 4 * c + i
            sib_copy(o).wait_recv()
            make_stream(1, o)

    def take_rows(p):
        first = 2 * p + 1
        row_copy(0, first, down).wait_recv()

        @pl.when(p < 7)
        def _():
            row_copy(first, first + 2, down).start()
            row_copy(0, first + 1, up).wait_recv()

            @pl.when(p < 6)
            def _():
                row_copy(first + 1, first + 3, up).start()

        make_weights(p, 0, first)
        make_weights(p, 1, (first + 1) % cols_n)

    def unit(u):
        m = jnp.where(u >= 9, 3, jnp.where(u >= 4, 2, jnp.where(u >= 1, 1, 0)))
        rest = u - m * m
        early = u < 16
        p = jnp.where(early, jnp.where(rest < m, rest, m), u // 4)
        c = jnp.where(early, jnp.where(rest < m, m, rest - m), u % 4)
        return p, c

    def prepare(u):
        for m in range(4):

            @pl.when(u == m * m)
            def _():
                take_rows(m)
                take_columns(m)

        @pl.when((u >= 16) & (u % 4 == 0) & (u < 32))
        def _():
            take_rows(u // 4)

    def products(u, tile):
        p, c = unit(u)
        place = pl.ds(pl.multiple_of(c * chunk, chunk), chunk)
        tile[...] = jnp.dot(stream[place, :], weights[p], preferred_element_type=f32)

    def apply(u, tile):
        p, c = unit(u)
        place = pl.ds(pl.multiple_of(c * chunk, chunk), chunk)
        sq = col_sq[place, :]
        exponent = tile[...] - jnp.concatenate([sq, sq], axis=1) - row_sq[p, 0:1, :]
        high, low = split(jnp.exp2(exponent))
        lhs = dirs[:, place]
        total[p] += jnp.dot(lhs, high, preferred_element_type=f32) + jnp.dot(lhs, low, preferred_element_type=f32)

    def finish(u):
        p, c = unit(u)

        @pl.when(c == 3)
        def _():
            both = total[p]
            both = both[0:rhs] + both[rhs : 2 * rhs]
            first = 2 * p + 1
            part[first] = both[:, 0:block]
            part[(first + 1) % cols_n] = both[:, block : 2 * block]

            @pl.when(p < 7)
            def _():
                part_copy(first, first + 1, (z + p + 1) % cols_n).start()
                part_copy(first + 1, first, (z + cols_n - p - 1) % cols_n).start()

            @pl.when(p == 7)
            def _():
                part_copy(15, 15, (z + 8) % cols_n).start()

    prepare(0)
    products(0, tile_a)

    @pl.loop(0, 16)
    def _(w):
        u = 2 * w
        prepare(u + 1)
        products(u + 1, tile_b)
        apply(u, tile_a)
        finish(u)
        prepare(u + 2)
        products(jnp.minimum(u + 2, 31), tile_a)
        apply(u + 1, tile_b)
        finish(u + 1)

    direction = dir_ref[...]
    residual = res_ref[...]
    applied = part[0] + noise_var * direction
    for slot in range(1, cols_n):
        part_copy(slot, slot, z).wait_recv()
        applied = applied + part_in[slot]

    lane = lax.broadcasted_iota(jnp.int32, (rhs, block), 1)
    line = lax.broadcasted_iota(jnp.int32, (rhs, block), 0)
    packed = jnp.zeros((rhs, block), f32)
    for q, values in enumerate((residual * residual, direction * applied, residual * applied, applied * applied)):
        packed = jnp.where(lane == line + q * rhs, jnp.sum(values, axis=1, keepdims=True), packed)
    stat_z[0] = jnp.sum(packed, axis=0, keepdims=True)

    def z_copy(step):
        return pltpu.make_async_remote_copy(
            src_ref=stat_z.at[0],
            dst_ref=stat_z.at[step],
            send_sem=sz_send.at[step],
            recv_sem=sz_recv.at[step],
            device_id=(r, (z + step) % cols_n),
            device_id_type=MESH,
        )

    def r_copy(step):
        return pltpu.make_async_remote_copy(
            src_ref=stat_r.at[0],
            dst_ref=stat_r.at[step],
            send_sem=sr_send.at[step],
            recv_sem=sr_recv.at[step],
            device_id=((r + step) % rows_n, z),
            device_id_type=MESH,
        )

    for step in range(1, cols_n):
        z_copy(step).start()
    for step in range(1, cols_n):
        z_copy(step).wait_recv()
    stat_r[0] = jnp.sum(stat_z[...], axis=0)
    for step in range(1, rows_n):
        r_copy(step).start()
    for step in range(1, rows_n):
        r_copy(step).wait_recv()
    sums = jnp.broadcast_to(jnp.sum(stat_r[...], axis=0), (rhs, block))

    def take(q):
        return jnp.sum(jnp.where(lane == line + q * rhs, sums, 0.0), axis=1, keepdims=True)

    norm_now, curvature, cross, square = take(0), take(1), take(2), take(3)
    step_size = norm_now / curvature
    norm_next = jnp.maximum(norm_now - step_size * (2.0 * cross - step_size * square), 0.0)
    ratio = norm_next / norm_now
    next_residual = residual - step_size * applied
    nsol_ref[...] = sol_ref[...] + step_size * direction
    nres_ref[...] = next_residual
    ndir_ref[...] = next_residual + ratio * direction

    for slot in range(1, cols_n):
        row_copy(0, slot, z).wait_send()
        part_copy(slot, slot, z).wait_send()
        z_copy(slot).wait_send()
    for o in range(plane):
        sib_copy(o).wait_send()
        if o > 0:
            col_copy(o).wait_send()
    for step in range(1, rows_n):
        r_copy(step).wait_send()


def per_device(points, solution, residual, direction):
    vmem = pl.BlockSpec(memory_space=pltpu.VMEM)
    dma = pltpu.SemaphoreType.DMA
    out = jax.ShapeDtypeStruct((rhs, block), f32)
    span = rows_n * block
    return pl.pallas_call(
        kernel,
        out_shape=(out, out, out),
        in_specs=[vmem] * 4,
        out_specs=(vmem, vmem, vmem),
        scratch_shapes=[
            pltpu.VMEM((2, plane, block + rhs, block), f32),
            pltpu.VMEM((cols_n, block, block), f32),
            pltpu.VMEM((pairs, 4 * block, 2 * block), bf16),
            pltpu.VMEM((pairs, 8, 2 * block), f32),
            pltpu.VMEM((span, 4 * block), bf16),
            pltpu.VMEM((span, block), f32),
            pltpu.VMEM((2 * rhs, span), bf16),
            pltpu.VMEM((chunk, 2 * block), f32),
            pltpu.VMEM((chunk, 2 * block), f32),
            pltpu.VMEM((pairs, 2 * rhs, 2 * block), f32),
            pltpu.VMEM((cols_n, rhs, block), f32),
            pltpu.VMEM((cols_n, rhs, block), f32),
            pltpu.VMEM((cols_n, 1, block), f32),
            pltpu.VMEM((rows_n, 1, block), f32),
            dma((plane,)),
            dma((plane,)),
            dma((plane,)),
            dma((plane,)),
            dma((cols_n,)),
            dma((cols_n,)),
            dma((cols_n,)),
            dma((cols_n,)),
            dma((cols_n,)),
            dma((cols_n,)),
            dma((rows_n,)),
            dma((rows_n,)),
        ],
        compiler_params=pltpu.CompilerParams(
            collective_id=0, has_side_effects=True, vmem_limit_bytes=48 * 1024 * 1024
        ),
        name="cg_step",
    )(points, solution, residual, direction)


def solution(mesh):
    spec = P(None, ("row", "col"))
    return jax.shard_map(
        per_device, mesh=mesh, in_specs=(spec,) * 4, out_specs=(spec,) * 3, check_vma=False
    )
```

time: 540 us -> 86.4 us (0.16)
  blocking collectives: 240 us -> 0 us
  waiting for transfers between devices: 167 us -> 0 us
  matrix products: 94.4 us -> 0 us
  Pallas kernels: 0 us -> 80.7 us
  between operations: 13.8 us -> 0.65 us
  other arithmetic: 12.3 us -> 0 us
    psum x2 -> x0, blocking collectives: 213 us -> none  [the longest x1 112 us: per_device(): lax.psum((jnp.sum(residual * residual, axis=1), jnp.sum(direction * appli...]
    all_gather x2 -> x0, waiting for transfers between devices: 109 us -> none  [the longest x1 69 us: per_device(): lax.all_gather(points, 'row', axis=1, tiled=True)]
    dot_general x16 -> x0, matrix products: 94.4 us -> none  [the longest x8 53.7 us: kernel_product(): lax.dot_general(pts_piece, rows_pts, (((0,), (0,)), ((), ())), precision=...]
    pallas_call x0 -> x1, Pallas kernels: none -> 80.7 us  [per_device(): pl.pallas_call(kernel, out_shape=(out, out, out), in_specs=[vmem] * 4, ou...]
    reduce_scatter x1 -> x0, waiting for transfers between devices: 56.3 us -> none  [per_device(): lax.psum_scatter(partial_value, 'col', scatter_dimension=1, tiled=True)]
    all_gather x1 -> x0, blocking collectives: 27.6 us -> none  [per_device(): lax.all_gather(direction, 'row', axis=1, tiled=True)]
    reduce_sum x12 -> x0, other arithmetic: 11.6 us -> none  [the longest x8 7.89 us: kernel_product(): piece_sq = jnp.sum(pts_piece * pts_piece, axis=0)]
  transfers between devices with their start and end apart: 3 -> 0, of which waited for: 3 -> 0; matrix products, arithmetic and copies ran while one was open for 0% -> 0% of each run, Pallas kernels for 0% -> 0%
where the time goes in v1:
time: 86.4 us; the launch traced here: 86.1 us
  Pallas kernels  80.7 us (93%)
  local copies, waits for them, and re-layouts  4.72 us (5%)
    pallas_call x1, Pallas kernels, per_device(): pl.pallas_call(kernel, out_shape=(out, out, out), in_specs=[vmem] * 4, ou...  80.7 us
    unnamed x11, local copies, waits for them, and re-layouts  4.72 us

profile of v1, /device:TPU:1, one launch (start us, length us, event | category | flops | bytes accessed | tf_op | source)
XLA Modules:
  0.0 86.1 jit_solution(14917757380473976140)
XLA Ops:
  0.6 0.0 copy-start
  0.6 0.8 copy-done
  1.5 0.0 copy-start.1
  1.5 0.7 copy-done.1
  2.2 0.0 copy-start.2
  2.2 0.7 copy-done.2
  2.9 0.0 copy-start.3
  2.9 0.7 copy-done.3
  3.6 80.7 %cg_step.1 = (f32[16,128]{1,0:T(8,128)S(1)}, f32[16,128]{1,0:T(8,128)S(1)}, f32[16,128]{1,0:T(8,128)S(1)}) custom-call(f32[128,128]{1,0:T(8,128)S(1)} %copy-done, f32[16,128]{1,0:T(8,128)S(1)} %copy-done.1, f32[16,128]{1,0:T(8,128)S(1)} %copy-done.2, f32[16,128]{1,0:T(8,128)S(1)} %copy-done.3), custom_call_target="tpu_custom_call" | custom-call | tf_op jit(solution)/shard_map/cg_step/pallas_call | solution.py:340
  84.3 0.6 copy.10
  84.9 0.6 copy.11
  85.5 0.6 copy.12
Async XLA Ops:
  0.6 0.8 copy-start
  1.5 0.7 copy-start.1
  2.2 0.7 copy-start.2
  2.9 0.7 copy-start.3

commit v2 on v1

--- a/solution.py
+++ b/solution.py
@@ -24,11 +24,39 @@
 chunk = 1024
 pairs = 8
 
-offsets = sorted(
-    [(dx, dy) for dx in range(side) for dy in range(side)],
-    key=lambda d: (min(d[0], side - d[0]) + min(d[1], side - d[1]), max(min(d[0], side - d[0]), min(d[1], side - d[1]))),
-)
+offsets = [
+    (0, 0), (1, 0), (3, 0), (0, 1),
+    (0, 3), (1, 1), (3, 3), (1, 3),
+    (3, 1), (2, 0), (0, 2), (2, 1),
+    (2, 3), (3, 2), (1, 2), (2, 2),
+]
 plane = len(offsets)
+near = [(1, 0), (3, 0), (0, 1), (0, 3)]
+diagonal = [(1, 1), (3, 3), (3, 1), (1, 3)]
+relays = {
+    (3, 0): [(3, 0)],
+    (0, 3): [(0, 3)],
+    (1, 1): [(1, 0), (1, 1)],
+    (3, 3): [(3, 0)],
+    (3, 1): [(0, 1)],
+    (1, 3): [(0, 3)],
+}
+far = [o for o in offsets if o not in near + diagonal + [(0, 0)]]
+
+units = [
+    (0, 0), (1, 0), (2, 0), (2, 1), (1, 1), (0, 1), (3, 0), (3, 1),
+    (4, 0), (4, 1), (2, 2), (3, 2), (4, 2), (2, 3), (3, 3), (4, 3),
+    (5, 0), (5, 1), (5, 2), (5, 3), (6, 0), (6, 1), (6, 2), (6, 3),
+    (7, 0), (7, 1), (7, 2), (7, 3), (1, 2), (1, 3), (0, 2), (0, 3),
+]
+
+
+def lookup(table, u):
+    value = table[0]
+    for i in range(1, len(table)):
+        if table[i] != table[i - 1]:
+            value = jnp.where(u >= i, table[i], value)
+    return value
 
 
 def split(values):
@@ -38,10 +66,10 @@
 
 
 def kernel(
-    pts_ref,
-    sol_ref,
-    res_ref,
-    dir_ref,
+    pts_hbm,
+    sol_hbm,
+    res_hbm,
+    dir_hbm,
     nsol_ref,
     nres_ref,
     ndir_ref,
@@ -59,6 +87,10 @@
     part_in,
     stat_z,
     stat_r,
+    sol_ref,
+    res_ref,
+    dir_ref,
+    load,
     col_send,
     col_recv,
     sib_send,
@@ -78,6 +110,14 @@
     sibling = r + 1 - 2 * core
     up, down = (z + 1) % cols_n, (z + cols_n - 1) % cols_n
 
+    loads = [
+        pltpu.make_async_copy(src, dst, load.at[i])
+        for i, (src, dst) in enumerate(
+            ((pts_hbm, row_in.at[0]), (dir_hbm, dir_ref), (res_hbm, res_ref), (sol_hbm, sol_ref))
+        )
+    ]
+    for copy in loads:
+        copy.start()
     barrier = pltpu.get_barrier_semaphore()
 
     @pl.loop(1, cols_n)
@@ -88,8 +128,9 @@
     def _(step):
         pl.semaphore_signal(barrier, inc=1, device_id=((r + step) % rows_n, z), device_id_type=MESH)
 
-    row_in[0] = pts_ref[...]
-    col_in[0, 0, 0:block, :] = pts_ref[...].T
+    for copy in loads:
+        copy.wait()
+    col_in[0, 0, 0:block, :] = row_in[0].T
     col_in[0, 0, block : block + rhs, :] = dir_ref[...]
     total[...] = jnp.zeros_like(total)
 
@@ -105,14 +146,17 @@
             device_id_type=MESH,
         )
 
-    def col_copy(o):
-        dx, dy = offsets[o]
-        target = (((x + side - dx) % side) * side + (y + side - dy) % side) * 2 + core
-        return pltpu.make_async_remote_copy(
-            src_ref=col_in.at[0, 0],
-            dst_ref=col_in.at[0, o],
-            send_sem=col_send.at[o],
-            recv_sem=col_recv.at[o],
+    def slot_of(offset):
+        return offsets.index((offset[0] % side, offset[1] % side))
+
+    def col_copy(offset, step):
+        target = (((x + side - step[0]) % side) * side + (y + side - step[1]) % side) * 2 + core
+        dst = slot_of((offset[0] + step[0], offset[1] + step[1]))
+        return pltpu.make_async_remote_copy(
+            src_ref=col_in.at[0, slot_of(offset)],
+            dst_ref=col_in.at[0, dst],
+            send_sem=col_send.at[dst],
+            recv_sem=col_recv.at[dst],
             device_id=(target, z),
             device_id_type=MESH,
         )
@@ -140,8 +184,8 @@
     row_copy(0, 1, down).start()
     row_copy(0, 2, up).start()
     sib_copy(0).start()
-    for o in range(1, plane):
-        col_copy(o).start()
+    for offset in near + diagonal:
+        col_copy((0, 0), offset).start()
 
     def make_weights(p, half, slot):
         pts = row_in[slot]
@@ -166,53 +210,80 @@
         dirs[0:rhs, place] = high
         dirs[rhs : 2 * rhs, place] = low
 
-    def take_columns(c):
+    def take_columns(arrived):
+        for offset in arrived:
+            col_copy((0, 0), offset).wait_recv()
+            for step in relays.get(offset, ()):
+                col_copy(offset, step).start()
+            sib_copy(slot_of(offset)).start()
+
+    def use_columns(c):
         for i in range(4):
-            o = 4 * c + i
-            if o > 0:
-                col_copy(o).wait_recv()
-                sib_copy(o).start()
-            make_stream(0, o)
+            make_stream(0, 4 * c + i)
         for i in range(4):
-            o = 4 * c + i
-            sib_copy(o).wait_recv()
-            make_stream(1, o)
-
-    def take_rows(p):
-        first = 2 * p + 1
-        row_copy(0, first, down).wait_recv()
-
-        @pl.when(p < 7)
-        def _():
-            row_copy(first, first + 2, down).start()
-            row_copy(0, first + 1, up).wait_recv()
-
-            @pl.when(p < 6)
-            def _():
-                row_copy(first + 1, first + 3, up).start()
-
-        make_weights(p, 0, first)
-        make_weights(p, 1, (first + 1) % cols_n)
+            sib_copy(4 * c + i).wait_recv()
+            make_stream(1, 4 * c + i)
+
+    onward = {1: (1, 2), 2: (2,), 3: (2,), 4: (2,), 6: (1, 2)}
+
+    def take_rows(d):
+        plus, minus = 2 * d - 1, 2 * d
+        row_copy(0, plus, z).wait_recv()
+        for step in onward.get(d, ()):
+            row_copy(plus, plus + 2 * step, (z + cols_n - step) % cols_n).start()
+        if d < 8:
+            row_copy(0, minus, z).wait_recv()
+            for step in onward.get(d, ()):
+                if d + step < 8:
+                    row_copy(minus, minus + 2 * step, (z + step) % cols_n).start()
+        make_weights(d - 1, 0, plus)
+        make_weights(d - 1, 1, minus % cols_n)
+
+    def event_0():
+        take_rows(1)
+        take_columns(near)
+        use_columns(0)
+
+    def event_1():
+        take_rows(2)
+
+    def event_2():
+        take_columns(diagonal)
+        take_rows(3)
+        use_columns(1)
+
+    def event_6():
+        take_rows(4)
+
+    def event_8():
+        take_rows(5)
+        take_columns(far)
+
+    def event_10():
+        use_columns(2)
+
+    def event_13():
+        use_columns(3)
+
+    events = {
+        1: event_1,
+        2: event_2,
+        6: event_6,
+        8: event_8,
+        10: event_10,
+        13: event_13,
+        16: lambda: take_rows(6),
+        20: lambda: take_rows(7),
+        24: lambda: take_rows(8),
+    }
 
     def unit(u):
-        m = jnp.where(u >= 9, 3, jnp.where(u >= 4, 2, jnp.where(u >= 1, 1, 0)))
-        rest = u - m * m
-        early = u < 16
-        p = jnp.where(early, jnp.where(rest < m, rest, m), u // 4)
-        c = jnp.where(early, jnp.where(rest < m, m, rest - m), u % 4)
-        return p, c
-
-    def prepare(u):
-        for m in range(4):
-
-            @pl.when(u == m * m)
-            def _():
-                take_rows(m)
-                take_columns(m)
-
-        @pl.when((u >= 16) & (u % 4 == 0) & (u < 32))
-        def _():
-            take_rows(u // 4)
+        return lookup([p for p, _ in units], u), lookup([c for _, c in units], u)
+
+    def prepare(u, parity):
+        for when, event in events.items():
+            if when % 2 == parity:
+                pl.when(u == when)(event)
 
     def products(u, tile):
         p, c = unit(u)
@@ -248,17 +319,17 @@
             def _():
                 part_copy(15, 15, (z + 8) % cols_n).start()
 
-    prepare(0)
+    event_0()
     products(0, tile_a)
 
     @pl.loop(0, 16)
     def _(w):
         u = 2 * w
-        prepare(u + 1)
+        prepare(u + 1, 1)
         products(u + 1, tile_b)
         apply(u, tile_a)
         finish(u)
-        prepare(u + 2)
+        prepare(u + 2, 0)
         products(jnp.minimum(u + 2, 31), tile_a)
         apply(u + 1, tile_b)
         finish(u + 1)
@@ -327,7 +398,7 @@
     for o in range(plane):
         sib_copy(o).wait_send()
         if o > 0:
-            col_copy(o).wait_send()
+            col_copy((0, 0), offsets[o]).wait_send()
     for step in range(1, rows_n):
         r_copy(step).wait_send()
 
@@ -340,7 +411,7 @@
     return pl.pallas_call(
         kernel,
         out_shape=(out, out, out),
-        in_specs=[vmem] * 4,
+        in_specs=[pl.BlockSpec(memory_space=pl.ANY)] * 4,
         out_specs=(vmem, vmem, vmem),
         scratch_shapes=[
             pltpu.VMEM((2, plane, block + rhs, block), f32),
@@ -357,6 +428,10 @@
             pltpu.VMEM((cols_n, rhs, block), f32),
             pltpu.VMEM((cols_n, 1, block), f32),
             pltpu.VMEM((rows_n, 1, block), f32),
+            pltpu.VMEM((rhs, block), f32),
+            pltpu.VMEM((rhs, block), f32),
+            pltpu.VMEM((rhs, block), f32),
+            dma((4,)),
             dma((plane,)),
             dma((plane,)),
             dma((plane,)),

time: 86.4 us -> 80.6 us (0.933)
  Pallas kernels: 80.7 us -> 75 us
    pallas_call x1, Pallas kernels: 80.7 us -> 75 us  [per_device(): pl.pallas_call(kernel, out_shape=(out, out, out), in_specs=[pl.BlockSpec(...]
where the time goes in v2:
time: 80.6 us; the launch traced here: 80.3 us
  Pallas kernels  75 us (93%)
  local copies, waits for them, and re-layouts  4.72 us (6%)
    pallas_call x1, Pallas kernels, per_device(): pl.pallas_call(kernel, out_shape=(out, out, out), in_specs=[pl.BlockSpec(...  75 us
    unnamed x11, local copies, waits for them, and re-layouts  4.72 us

profile of v2, /device:TPU:1, one launch (start us, length us, event | category | flops | bytes accessed | tf_op | source)
XLA Modules:
  0.0 80.3 jit_solution(10772926123572004389)
XLA Ops:
  0.6 0.0 copy-start
  0.6 0.8 %copy-done = f32[128,128]{1,0:T(8,128)S(1)} copy-done((f32[128,128]{1,0:T(8,128)S(1)}, f32[128,128]{1,0:T(8,128)}, u32[]{:S(2)}) %copy-start) | copy-done | bytes 65560
  1.5 0.0 copy-start.1
  1.5 0.7 copy-done.1
  2.2 0.0 copy-start.2
  2.2 0.7 copy-done.2
  2.9 0.0 copy-start.3
  2.9 0.7 copy-done.3
  3.6 75.0 %cg_step.1 = (f32[16,128]{1,0:T(8,128)S(1)}, f32[16,128]{1,0:T(8,128)S(1)}, f32[16,128]{1,0:T(8,128)S(1)}) custom-call(f32[128,128]{1,0:T(8,128)S(1)} %copy-done, f32[16,128]{1,0:T(8,128)S(1)} %copy-done.1, f32[16,128]{1,0:T(8,128)S(1)} %copy-done.2, f32[16,128]{1,0:T(8,128)S(1)} %copy-done.3), custom_call_target="tpu_custom_call" | custom-call | tf_op jit(solution)/shard_map/cg_step/pallas_call | solution.py:411
  78.5 0.6 copy.10
  79.1 0.6 copy.11
  79.7 0.6 copy.12
Async XLA Ops:
  0.6 0.8 %copy-start = (f32[128,128]{1,0:T(8,128)S(1)}, f32[128,128]{1,0:T(8,128)}, u32[]{:S(2)}) copy-start(f32[128,128]{1,0:T(8,128)} %pts_hbm.1) | copy-start | bytes 196612
  1.5 0.7 copy-start.1
  2.2 0.7 copy-start.2
  2.9 0.7 copy-start.3

commit v3 on v2

v3 whole, which is shorter than its diff:
```python
import math

import jax
import jax.numpy as jnp
from jax import lax
from jax.experimental import pallas as pl
from jax.experimental.pallas import tpu as pltpu
from jax.sharding import PartitionSpec as P

noise_var = 0.5
inv_two_len = 0.03125
scale = inv_two_len * math.log2(math.e)

MESH = pl.DeviceIdType.MESH
f32 = jnp.float32
bf16 = jnp.bfloat16

side = 4
rows_n = 32
cols_n = 16
block = 128
rhs = 16
chunk = 1024
chunks = 4
pairs = 4
held = 9

offsets = [
    (0, 0), (1, 0), (3, 0), (0, 1),
    (0, 3), (1, 1), (3, 3), (1, 3),
    (3, 1), (2, 0), (0, 2), (2, 1),
    (2, 3), (3, 2), (1, 2), (2, 2),
]
plane = len(offsets)
near = [(1, 0), (3, 0), (0, 1), (0, 3)]
diagonal = [(1, 1), (3, 3), (3, 1), (1, 3)]
far = [o for o in offsets if o not in near + diagonal + [(0, 0)]]
relays = {
    (3, 0): [(3, 0)],
    (0, 3): [(0, 3)],
    (1, 1): [(1, 0), (1, 1)],
    (3, 3): [(3, 0)],
    (3, 1): [(0, 1)],
    (1, 3): [(0, 3)],
}

units = [
    (0, 0), (1, 0), (0, 1), (1, 1), (2, 0), (2, 1), (3, 0), (3, 1),
    (3, 2), (2, 2), (1, 2), (0, 2), (3, 3), (2, 3), (1, 3), (0, 3),
]


def lookup(table, u):
    value = table[0]
    for i in range(1, len(table)):
        if table[i] != table[i - 1]:
            value = jnp.where(u >= i, table[i], value)
    return value


def slot_of(offset):
    return offsets.index((offset[0] % side, offset[1] % side))


def split(values):
    high = values.astype(bf16)
    low = (values - high.astype(f32)).astype(bf16)
    return high, low


def dot(a, b):
    return jnp.dot(a, b, preferred_element_type=f32)


def dot_turned(a, b):
    return lax.dot_general(a, b, (((1,), (1,)), ((), ())), preferred_element_type=f32)


def kernel(
    pts_hbm,
    sol_hbm,
    res_hbm,
    dir_hbm,
    nsol_ref,
    nres_ref,
    ndir_ref,
    col_in,
    row_in,
    weights,
    row_sq,
    row_dirs,
    stream,
    col_sq,
    dirs,
    own_weights,
    own_sq,
    tile_a,
    tile_b,
    own_a,
    own_b,
    row_total,
    col_total,
    own_total,
    part,
    part_in,
    col_part,
    col_part_in,
    stat_z,
    stat_r,
    sol_ref,
    res_ref,
    load,
    col_send,
    col_recv,
    sib_send,
    sib_recv,
    row_send,
    row_recv,
    part_send,
    part_recv,
    cp_send,
    cp_recv,
    sz_send,
    sz_recv,
    sr_send,
    sr_recv,
):
    r = lax.axis_index("row")
    z = lax.axis_index("col")
    x, y, core = r // 8, (r // 2) % 4, r % 2
    sibling = r + 1 - 2 * core

    loads = [
        pltpu.make_async_copy(src, dst, load.at[i])
        for i, (src, dst) in enumerate(
            (
                (pts_hbm, row_in.at[0, 0:block]),
                (dir_hbm, row_in.at[0, block : block + rhs]),
                (res_hbm, res_ref),
                (sol_hbm, sol_ref),
            )
        )
    ]
    for copy in loads:
        copy.start()

    barrier = pltpu.get_barrier_semaphore()
    for step in (4, 12, 3, 13, 2, 14, 1, 15):
        pl.semaphore_signal(barrier, inc=1, device_id=(r, (z + step) % cols_n), device_id_type=MESH)

    @pl.loop(1, rows_n)
    def _(step):
        pl.semaphore_signal(barrier, inc=1, device_id=((r + step) % rows_n, z), device_id_type=MESH)

    for copy in loads:
        copy.wait()
    col_in[0, 0, 0:block, :] = row_in[0, 0:block, :].T
    col_in[0, 0, block : block + rhs, :] = row_in[0, block : block + rhs, :]
    row_total[...] = jnp.zeros_like(row_total)
    col_total[...] = jnp.zeros_like(col_total)
    own_total[...] = jnp.zeros_like(own_total)

    pl.semaphore_wait(barrier, 8 + rows_n - 1)

    def row_copy(src, dst, step):
        return pltpu.make_async_remote_copy(
            src_ref=row_in.at[src],
            dst_ref=row_in.at[dst],
            send_sem=row_send.at[dst],
            recv_sem=row_recv.at[dst],
            device_id=(r, (z + cols_n + step) % cols_n),
            device_id_type=MESH,
        )

    def device_at(offset, other):
        target = (((x + offset[0]) % side) * side + (y + offset[1]) % side) * 2
        return target + (1 - core if other else core)

    def col_copy(offset, step):
        dst = slot_of((offset[0] + step[0], offset[1] + step[1]))
        return pltpu.make_async_remote_copy(
            src_ref=col_in.at[0, slot_of(offset)],
            dst_ref=col_in.at[0, dst],
            send_sem=col_send.at[dst],
            recv_sem=col_recv.at[dst],
            device_id=(device_at((side - step[0], side - step[1]), False), z),
            device_id_type=MESH,
        )

    def sib_copy(o):
        return pltpu.make_async_remote_copy(
            src_ref=col_in.at[0, o],
            dst_ref=col_in.at[1, o],
            send_sem=sib_send.at[o],
            recv_sem=sib_recv.at[o],
            device_id=(sibling, z),
            device_id_type=MESH,
        )

    def part_copy(k):
        return pltpu.make_async_remote_copy(
            src_ref=part.at[k],
            dst_ref=part_in.at[k],
            send_sem=part_send.at[k],
            recv_sem=part_recv.at[k],
            device_id=(r, (z + (cols_n - k if k % 2 else k)) % cols_n),
            device_id_type=MESH,
        )

    def col_part_copy(b, o):
        dx, dy = offsets[o]
        dst = slot_of((-dx, -dy))
        return pltpu.make_async_remote_copy(
            src_ref=col_part.at[b, o],
            dst_ref=col_part_in.at[b, dst],
            send_sem=cp_send.at[b, o],
            recv_sem=cp_recv.at[b, dst],
            device_id=(device_at((dx, dy), b == 1), z),
            device_id_type=MESH,
        )

    row_copy(0, 3, 3).start()
    row_copy(0, 4, -4).start()
    row_copy(0, 1, 1).start()
    row_copy(0, 2, -2).start()
    sib_copy(0).start()
    for offset in near + diagonal:
        col_copy((0, 0), offset).start()

    def turn(pts):
        high, low = split(pts * (2.0 * scale))
        stacked = jnp.concatenate([high, low, high, low], axis=0)
        return stacked, jnp.broadcast_to(scale * jnp.sum(pts * pts, axis=0, keepdims=True), (8, block))

    def make_weights(p):
        for half in range(2):
            k = 2 * p + 1 + half
            lanes = slice(half * block, (half + 1) * block)
            weights[p, :, lanes], row_sq[p, :, lanes] = turn(row_in[k, 0:block, :])
            if k < 8:
                high, low = split(row_in[k, block : block + rhs, :])
            else:
                high = low = jnp.zeros((rhs, block), bf16)
            row_dirs[p, 0:rhs, lanes] = high
            row_dirs[p, rhs : 2 * rhs, lanes] = low

    def make_stream(b, o):
        place = pl.ds(pl.multiple_of((2 * o + b) * block, block), block)
        pts = col_in[b, o, 0:block, :]
        high, low = split(pts)
        stream[place, 0 * block : 1 * block] = high
        stream[place, 1 * block : 2 * block] = high
        stream[place, 2 * block : 3 * block] = low
        stream[place, 3 * block : 4 * block] = low
        col_sq[place, :] = jnp.broadcast_to(scale * jnp.sum(pts * pts, axis=1, keepdims=True), (block, block))
        high, low = split(col_in[b, o, block : block + rhs, :])
        dirs[0:rhs, place] = high
        dirs[rhs : 2 * rhs, place] = low

    def take_columns(arrived):
        for offset in arrived:
            col_copy((0, 0), offset).wait_recv()
            for step in relays.get(offset, ()):
                col_copy(offset, step).start()
            sib_copy(slot_of(offset)).start()

    def use_columns(c):
        @pl.loop(4 * c, 4 * c + 4)
        def _(o):
            make_stream(0, o)

        @pl.loop(4 * c, 4 * c + 4)
        def _(o):
            sib_copy(o).wait_recv()
            make_stream(1, o)

    def take_row(k):
        row_copy(0, k, 0).wait_recv()
        if k == 3:
            row_copy(3, 5, 2).start()
            row_copy(3, 7, 4).start()
        if k == 4:
            row_copy(4, 6, -2).start()
            row_copy(4, 8, -4).start()

    def event_0():
        take_columns(near)
        take_row(1)
        take_row(2)
        make_weights(0)
        take_row(3)
        take_row(4)
        use_columns(0)

    def event_1():
        make_weights(1)

    def event_2():
        take_columns(diagonal)
        use_columns(1)

    def event_4():
        take_row(5)
        take_row(6)
        make_weights(2)

    def event_6():
        take_row(7)
        take_row(8)
        make_weights(3)

    def event_7():
        take_columns(far)

    def event_8():
        use_columns(2)

    def event_12():
        use_columns(3)

    events = {1: event_1, 2: event_2, 4: event_4, 6: event_6, 7: event_7, 8: event_8, 12: event_12}

    def send_rows(p):
        both = row_total[p]
        both = both[0:rhs] + both[rhs : 2 * rhs]
        for half in range(2):
            k = 2 * p + 1 + half
            part[k] = both[:, half * block : (half + 1) * block]
            part_copy(k).start()

    def send_columns(c):
        for o in range(4 * c, 4 * c + 4):
            for b in range(2):
                place = slice((2 * o + b) * block, (2 * o + b + 1) * block)
                col_part[b, o] = col_total[0:rhs, place] + col_total[rhs : 2 * rhs, place]
                if (b, o) != (0, 0):
                    col_part_copy(b, o).start()

    def finish_7():
        send_columns(0)
        send_columns(1)

    def finish_15():
        send_columns(3)
        send_rows(0)

    finishes = {
        7: finish_7,
        11: lambda: send_columns(2),
        12: lambda: send_rows(3),
        13: lambda: send_rows(2),
        14: lambda: send_rows(1),
        15: finish_15,
    }

    def unit(u):
        return lookup([p for p, _ in units], u), lookup([c for _, c in units], u)

    def run(table, u, parity):
        for when, event in table.items():
            if when % 2 == parity:
                pl.when(u == when)(event)

    def products(u, tile):
        p, c = unit(u)
        place = pl.ds(pl.multiple_of(c * chunk, chunk), chunk)
        tile[...] = dot(stream[place, :], weights[p])

    def apply(u, tile):
        p, c = unit(u)
        place = pl.ds(pl.multiple_of(c * chunk, chunk), chunk)
        sq = col_sq[place, :]
        exponent = tile[...] - jnp.concatenate([sq, sq], axis=1) - row_sq[p, 0:1, :]
        high, low = split(jnp.exp2(exponent))
        row_total[p] += dot(dirs[:, place], high) + dot(dirs[:, place], low)
        col_total[:, place] += dot_turned(row_dirs[p], high) + dot_turned(row_dirs[p], low)

    event_0()
    products(0, tile_a)

    @pl.loop(0, len(units) // 2)
    def _(w):
        u = 2 * w
        run(events, u + 1, 1)
        products(u + 1, tile_b)
        apply(u, tile_a)
        run(finishes, u, 0)
        run(events, u + 2, 0)
        products(jnp.minimum(u + 2, len(units) - 1), tile_a)
        apply(u + 1, tile_b)
        run(finishes, u + 1, 1)

    own_weights[...], own_sq[...] = turn(row_in[0, 0:block, :])

    def own_products(c, tile):
        place = pl.ds(pl.multiple_of(c * chunk, chunk), chunk)
        tile[...] = dot(stream[place, :], own_weights[...])

    def own_apply(c, tile):
        place = pl.ds(pl.multiple_of(c * chunk, chunk), chunk)
        high, low = split(jnp.exp2(tile[...] - col_sq[place, :] - own_sq[0:1, :]))
        own_total[...] += dot(dirs[:, place], high) + dot(dirs[:, place], low)

    own_products(0, own_a)

    @pl.loop(0, chunks // 2)
    def _(w):
        c = 2 * w
        own_products(c + 1, own_b)
        own_apply(c, own_a)
        own_products(jnp.minimum(c + 2, chunks - 1), own_a)
        own_apply(c + 1, own_b)

    direction = row_in[0, block : block + rhs, :]
    residual = res_ref[...]
    applied = own_total[0:rhs] + own_total[rhs : 2 * rhs] + col_part[0, 0] + noise_var * direction
    for k in range(8, 0, -1):
        part_copy(k).wait_recv()
        applied = applied + part_in[k]
    for o in range(plane):
        for b in range(2):
            if (b, o) != (0, 0):
                col_part_copy(b, o).wait_recv()
                applied = applied + col_part_in[b, slot_of((-offsets[o][0], -offsets[o][1]))]

    lane = lax.broadcasted_iota(jnp.int32, (rhs, block), 1)
    line = lax.broadcasted_iota(jnp.int32, (rhs, block), 0)
    packed = jnp.zeros((rhs, block), f32)
    for q, values in enumerate((residual * residual, direction * applied, residual * applied, applied * applied)):
        packed = jnp.where(lane == line + q * rhs, jnp.sum(values, axis=1, keepdims=True), packed)
    stat_z[0] = jnp.sum(packed, axis=0, keepdims=True)

    def z_copy(step):
        return pltpu.make_async_remote_copy(
            src_ref=stat_z.at[0],
            dst_ref=stat_z.at[step],
            send_sem=sz_send.at[step],
            recv_sem=sz_recv.at[step],
            device_id=(r, (z + step) % cols_n),
            device_id_type=MESH,
        )

    def r_copy(step):
        return pltpu.make_async_remote_copy(
            src_ref=stat_r.at[0],
            dst_ref=stat_r.at[step],
            send_sem=sr_send.at[step],
            recv_sem=sr_recv.at[step],
            device_id=((r + step) % rows_n, z),
            device_id_type=MESH,
        )

    for step in sorted(range(1, cols_n), key=lambda step: -min(step, cols_n - step)):
        z_copy(step).start()
    for step in range(1, cols_n):
        z_copy(step).wait_recv()
    stat_r[0] = jnp.sum(stat_z[...], axis=0)
    for step in range(1, rows_n):
        r_copy(step).start()
    for step in range(1, rows_n):
        r_copy(step).wait_recv()
    sums = jnp.broadcast_to(jnp.sum(stat_r[...], axis=0), (rhs, block))

    def take(q):
        return jnp.sum(jnp.where(lane == line + q * rhs, sums, 0.0), axis=1, keepdims=True)

    norm_now, curvature, cross, square = take(0), take(1), take(2), take(3)
    step_size = norm_now / curvature
    norm_next = jnp.maximum(norm_now - step_size * (2.0 * cross - step_size * square), 0.0)
    ratio = norm_next / norm_now
    next_residual = residual - step_size * applied
    nsol_ref[...] = sol_ref[...] + step_size * direction
    nres_ref[...] = next_residual
    ndir_ref[...] = next_residual + ratio * direction

    for k in range(1, held):
        row_copy(0, k, 0).wait_send()
        part_copy(k).wait_send()
    for step in range(1, cols_n):
        z_copy(step).wait_send()
    for step in range(1, rows_n):
        r_copy(step).wait_send()
    for o in range(plane):
        sib_copy(o).wait_send()
        if o > 0:
            col_copy((0, 0), offsets[o]).wait_send()
        for b in range(2):
            if (b, o) != (0, 0):
                col_part_copy(b, o).wait_send()


def per_device(points, solution, residual, direction):
    vmem = pl.BlockSpec(memory_space=pltpu.VMEM)
    dma = pltpu.SemaphoreType.DMA
    out = jax.ShapeDtypeStruct((rhs, block), f32)
    span = rows_n * block
    return pl.pallas_call(
        kernel,
        out_shape=(out, out, out),
        in_specs=[pl.BlockSpec(memory_space=pltpu.HBM)] * 4,
        out_specs=(vmem, vmem, vmem),
        scratch_shapes=[
            pltpu.VMEM((2, plane, block + rhs, block), f32),
            pltpu.VMEM((held, block + rhs, block), f32),
            pltpu.VMEM((pairs, 4 * block, 2 * block), bf16),
            pltpu.VMEM((pairs, 8, 2 * block), f32),
            pltpu.VMEM((pairs, 2 * rhs, 2 * block), bf16),
            pltpu.VMEM((span, 4 * block), bf16),
            pltpu.VMEM((span, block), f32),
            pltpu.VMEM((2 * rhs, span), bf16),
            pltpu.VMEM((4 * block, block), bf16),
            pltpu.VMEM((8, block), f32),
            pltpu.VMEM((chunk, 2 * block), f32),
            pltpu.VMEM((chunk, 2 * block), f32),
            pltpu.VMEM((chunk, block), f32),
            pltpu.VMEM((chunk, block), f32),
            pltpu.VMEM((pairs, 2 * rhs, 2 * block), f32),
            pltpu.VMEM((2 * rhs, span), f32),
            pltpu.VMEM((2 * rhs, block), f32),
            pltpu.VMEM((held, rhs, block), f32),
            pltpu.VMEM((held, rhs, block), f32),
            pltpu.VMEM((2, plane, rhs, block), f32),
            pltpu.VMEM((2, plane, rhs, block), f32),
            pltpu.VMEM((cols_n, 1, block), f32),
            pltpu.VMEM((rows_n, 1, block), f32),
            pltpu.VMEM((rhs, block), f32),
            pltpu.VMEM((rhs, block), f32),
            dma((4,)),
            dma((plane,)),
            dma((plane,)),
            dma((plane,)),
            dma((plane,)),
            dma((held,)),
            dma((held,)),
            dma((held,)),
            dma((held,)),
            dma((2, plane)),
            dma((2, plane)),
            dma((cols_n,)),
            dma((cols_n,)),
            dma((rows_n,)),
            dma((rows_n,)),
        ],
        compiler_params=pltpu.CompilerParams(
            collective_id=0, has_side_effects=True, vmem_limit_bytes=60 * 1024 * 1024
        ),
        name="cg_step",
    )(points, solution, residual, direction)


def solution(mesh):
    spec = P(None, ("row", "col"))
    return jax.shard_map(
        per_device, mesh=mesh, in_specs=(spec,) * 4, out_specs=(spec,) * 3, check_vma=False
    )
```

time: 80.6 us -> 75.5 us (0.937)
  Pallas kernels: 75 us -> 72 us
  local copies, waits for them, and re-layouts: 4.72 us -> 2.6 us
    pallas_call x1, Pallas kernels: 75 us -> 72 us  [per_device(): pl.pallas_call(kernel, out_shape=(out, out, out), in_specs=[pl.BlockSpec(...]
    unnamed x11 -> x7, local copies, waits for them, and re-layouts: 4.72 us -> 2.6 us
where the time goes in v3:
time: 75.5 us; the launch traced here: 75.2 us
  Pallas kernels  72 us (95%)
  local copies, waits for them, and re-layouts  2.6 us (3%)
    pallas_call x1, Pallas kernels, per_device(): pl.pallas_call(kernel, out_shape=(out, out, out), in_specs=[pl.BlockSpec(...  72 us
    unnamed x7, local copies, waits for them, and re-layouts  2.6 us

profile of v3, /device:TPU:1, one launch (start us, length us, event | category | flops | bytes accessed | tf_op | source)
XLA Modules:
  0.0 75.2 jit_solution(11295954321956787800)
XLA Ops:
  0.6 72.0 %cg_step.1 = (f32[16,128]{1,0:T(8,128)}, f32[16,128]{1,0:T(8,128)}, f32[16,128]{1,0:T(8,128)}) custom-call(f32[128,128]{1,0:T(8,128)} %pts_hbm.1, f32[16,128]{1,0:T(8,128)} %sol_hbm.1, f32[16,128]{1,0:T(8,128)} %res_hbm.1, f32[16,128]{1,0:T(8,128)} %dir_hbm.1), custom_call_target="tpu_custom_call" | custom-call | tf_op jit(solution)/shard_map/cg_step/pallas_call | solution.py:497
  72.6 0.0 copy-start.1
  72.6 1.3 %copy.10 = f32[16,128]{1,0:T(8,128)} copy(f32[16,128]{1,0:T(8,128)} %get-tuple-element.6) | data formatting | bytes 16384
  73.9 0.0 copy-done.1
  73.9 0.0 copy-start
  73.9 0.6 copy.11
  74.5 0.1 copy-done
  74.6 0.6 copy.12
Async XLA Ops:
  72.6 1.3 %copy-start.1 = (f32[16,128]{1,0:T(8,128)S(1)}, f32[16,128]{1,0:T(8,128)}, u32[]{:S(2)}) copy-start(f32[16,128]{1,0:T(8,128)} %get-tuple-element.7) | copy-start | bytes 24580
  73.9 0.7 copy-start

commit v4 on v3

--- a/solution.py
+++ b/solution.py
@@ -45,8 +45,8 @@
 }
 
 units = [
-    (0, 0), (1, 0), (0, 1), (1, 1), (2, 0), (2, 1), (3, 0), (3, 1),
-    (3, 2), (2, 2), (1, 2), (0, 2), (3, 3), (2, 3), (1, 3), (0, 3),
+    (0, 0), (0, 1), (1, 0), (1, 1), (1, 2), (1, 3), (0, 2), (0, 3),
+    (2, 0), (2, 1), (2, 2), (2, 3), (3, 0), (3, 1), (3, 2), (3, 3),
 ]
 
 
@@ -219,8 +219,6 @@
             device_id_type=MESH,
         )
 
-    row_copy(0, 3, 3).start()
-    row_copy(0, 4, -4).start()
     row_copy(0, 1, 1).start()
     row_copy(0, 2, -2).start()
     sib_copy(0).start()
@@ -265,60 +263,55 @@
             sib_copy(slot_of(offset)).start()
 
     def use_columns(c):
-        @pl.loop(4 * c, 4 * c + 4)
-        def _(o):
+        for o in range(4 * c, 4 * c + 4):
             make_stream(0, o)
-
-        @pl.loop(4 * c, 4 * c + 4)
-        def _(o):
+        for o in range(4 * c, 4 * c + 4):
             sib_copy(o).wait_recv()
+        for o in range(4 * c, 4 * c + 4):
             make_stream(1, o)
 
     def take_row(k):
         row_copy(0, k, 0).wait_recv()
-        if k == 3:
-            row_copy(3, 5, 2).start()
-            row_copy(3, 7, 4).start()
-        if k == 4:
-            row_copy(4, 6, -2).start()
-            row_copy(4, 8, -4).start()
+        if k + 2 < held:
+            row_copy(k, k + 2, 2 if k % 2 else -2).start()
 
     def event_0():
+        take_row(1)
         take_columns(near)
-        take_row(1)
         take_row(2)
         make_weights(0)
+        use_columns(0)
+
+    def event_1():
+        take_columns(diagonal)
         take_row(3)
+        use_columns(1)
+
+    def event_2():
         take_row(4)
-        use_columns(0)
-
-    def event_1():
         make_weights(1)
 
-    def event_2():
-        take_columns(diagonal)
-        use_columns(1)
-
     def event_4():
+        own_units(0)
+        take_columns(far)
         take_row(5)
+        use_columns(2)
+
+    def event_5():
+        use_columns(3)
+
+    def event_6():
         take_row(6)
+
+    def event_8():
         make_weights(2)
 
-    def event_6():
+    def event_12():
         take_row(7)
         take_row(8)
         make_weights(3)
 
-    def event_7():
-        take_columns(far)
-
-    def event_8():
-        use_columns(2)
-
-    def event_12():
-        use_columns(3)
-
-    events = {1: event_1, 2: event_2, 4: event_4, 6: event_6, 7: event_7, 8: event_8, 12: event_12}
+    events = {1: event_1, 2: event_2, 4: event_4, 5: event_5, 6: event_6, 8: event_8, 12: event_12}
 
     def send_rows(p):
         both = row_total[p]
@@ -336,20 +329,17 @@
                 if (b, o) != (0, 0):
                     col_part_copy(b, o).start()
 
-    def finish_7():
-        send_columns(0)
-        send_columns(1)
-
     def finish_15():
+        send_rows(3)
         send_columns(3)
-        send_rows(0)
 
     finishes = {
-        7: finish_7,
-        11: lambda: send_columns(2),
-        12: lambda: send_rows(3),
-        13: lambda: send_rows(2),
-        14: lambda: send_rows(1),
+        5: lambda: send_rows(1),
+        7: lambda: send_rows(0),
+        11: lambda: send_rows(2),
+        12: lambda: send_columns(0),
+        13: lambda: send_columns(1),
+        14: lambda: send_columns(2),
         15: finish_15,
     }
 
@@ -374,6 +364,23 @@
         high, low = split(jnp.exp2(exponent))
         row_total[p] += dot(dirs[:, place], high) + dot(dirs[:, place], low)
         col_total[:, place] += dot_turned(row_dirs[p], high) + dot_turned(row_dirs[p], low)
+
+    own_weights[...], own_sq[...] = turn(row_in[0, 0:block, :])
+
+    def own_products(c, tile):
+        place = pl.ds(c * chunk, chunk)
+        tile[...] = dot(stream[place, :], own_weights[...])
+
+    def own_apply(c, tile):
+        place = pl.ds(c * chunk, chunk)
+        high, low = split(jnp.exp2(tile[...] - col_sq[place, :] - own_sq[0:1, :]))
+        own_total[...] += dot(dirs[:, place], high) + dot(dirs[:, place], low)
+
+    def own_units(c):
+        own_products(c, own_a)
+        own_products(c + 1, own_b)
+        own_apply(c, own_a)
+        own_apply(c + 1, own_b)
 
     event_0()
     products(0, tile_a)
@@ -390,26 +397,7 @@
         apply(u + 1, tile_b)
         run(finishes, u + 1, 1)
 
-    own_weights[...], own_sq[...] = turn(row_in[0, 0:block, :])
-
-    def own_products(c, tile):
-        place = pl.ds(pl.multiple_of(c * chunk, chunk), chunk)
-        tile[...] = dot(stream[place, :], own_weights[...])
-
-    def own_apply(c, tile):
-        place = pl.ds(pl.multiple_of(c * chunk, chunk), chunk)
-        high, low = split(jnp.exp2(tile[...] - col_sq[place, :] - own_sq[0:1, :]))
-        own_total[...] += dot(dirs[:, place], high) + dot(dirs[:, place], low)
-
-    own_products(0, own_a)
-
-    @pl.loop(0, chunks // 2)
-    def _(w):
-        c = 2 * w
-        own_products(c + 1, own_b)
-        own_apply(c, own_a)
-        own_products(jnp.minimum(c + 2, chunks - 1), own_a)
-        own_apply(c + 1, own_b)
+    own_units(2)
 
     direction = row_in[0, block : block + rhs, :]
     residual = res_ref[...]

time: 75.5 us -> 68.4 us (0.906)
  Pallas kernels: 72 us -> 64.9 us
    pallas_call x1, Pallas kernels: 72 us -> 64.9 us  [per_device(): pl.pallas_call(kernel, out_shape=(out, out, out), in_specs=[pl.BlockSpec(...]
where the time goes in v4:
time: 68.4 us; the launch traced here: 68.2 us
  Pallas kernels  64.9 us (95%)
  local copies, waits for them, and re-layouts  2.6 us (4%)
    pallas_call x1, Pallas kernels, per_device(): pl.pallas_call(kernel, out_shape=(out, out, out), in_specs=[pl.BlockSpec(...  64.9 us
    unnamed x7, local copies, waits for them, and re-layouts  2.6 us

profile of v4, /device:TPU:1, one launch (start us, length us, event | category | flops | bytes accessed | tf_op | source)
XLA Modules:
  0.0 68.2 jit_solution(13285762849904620762)
XLA Ops:
  0.6 64.9 %cg_step.1 = (f32[16,128]{1,0:T(8,128)}, f32[16,128]{1,0:T(8,128)}, f32[16,128]{1,0:T(8,128)}) custom-call(f32[128,128]{1,0:T(8,128)} %pts_hbm.1, f32[16,128]{1,0:T(8,128)} %sol_hbm.1, f32[16,128]{1,0:T(8,128)} %res_hbm.1, f32[16,128]{1,0:T(8,128)} %dir_hbm.1), custom_call_target="tpu_custom_call" | custom-call | tf_op jit(solution)/shard_map/cg_step/pallas_call | solution.py:485
  65.6 0.0 copy-start.1
  65.6 1.3 %copy.10 = f32[16,128]{1,0:T(8,128)} copy(f32[16,128]{1,0:T(8,128)} %get-tuple-element.6) | data formatting | bytes 16384
  66.9 0.0 copy-done.1
  66.9 0.0 copy-start
  66.9 0.6 copy.11
  67.5 0.1 copy-done
  67.6 0.6 copy.12
Async XLA Ops:
  65.6 1.3 %copy-start.1 = (f32[16,128]{1,0:T(8,128)S(1)}, f32[16,128]{1,0:T(8,128)}, u32[]{:S(2)}) copy-start(f32[16,128]{1,0:T(8,128)} %get-tuple-element.7) | copy-start | bytes 24580
  66.9 0.7 %copy-start = (f32[16,128]{1,0:T(8,128)S(1)}, f32[16,128]{1,0:T(8,128)}, u32[]{:S(2)}) copy-start(f32[16,128]{1,0:T(8,128)} %get-tuple-element.8) | copy-start | bytes 24580

commit v5 on v4

--- a/solution.py
+++ b/solution.py
@@ -24,6 +24,7 @@
 chunks = 4
 pairs = 4
 held = 9
+half_rows = (block + rhs) // 2
 
 offsets = [
     (0, 0), (1, 0), (3, 0), (0, 1),
@@ -44,20 +45,6 @@
     (1, 3): [(0, 3)],
 }
 
-units = [
-    (0, 0), (0, 1), (1, 0), (1, 1), (1, 2), (1, 3), (0, 2), (0, 3),
-    (2, 0), (2, 1), (2, 2), (2, 3), (3, 0), (3, 1), (3, 2), (3, 3),
-]
-
-
-def lookup(table, u):
-    value = table[0]
-    for i in range(1, len(table)):
-        if table[i] != table[i - 1]:
-            value = jnp.where(u >= i, table[i], value)
-    return value
-
-
 def slot_of(offset):
     return offsets.index((offset[0] % side, offset[1] % side))
 
@@ -78,12 +65,11 @@
 
 def kernel(
     pts_hbm,
-    sol_hbm,
     res_hbm,
     dir_hbm,
-    nsol_ref,
-    nres_ref,
-    ndir_ref,
+    applied_ref,
+    step_ref,
+    ratio_ref,
     col_in,
     row_in,
     weights,
@@ -107,7 +93,6 @@
     col_part_in,
     stat_z,
     stat_r,
-    sol_ref,
     res_ref,
     load,
     col_send,
@@ -130,6 +115,10 @@
     x, y, core = r // 8, (r // 2) % 4, r % 2
     sibling = r + 1 - 2 * core
 
+    def device_at(offset, other):
+        target = (((x + offset[0]) % side) * side + (y + offset[1]) % side) * 2
+        return target + (1 - core if other else core)
+
     loads = [
         pltpu.make_async_copy(src, dst, load.at[i])
         for i, (src, dst) in enumerate(
@@ -137,7 +126,6 @@
                 (pts_hbm, row_in.at[0, 0:block]),
                 (dir_hbm, row_in.at[0, block : block + rhs]),
                 (res_hbm, res_ref),
-                (sol_hbm, sol_ref),
             )
         )
     ]
@@ -145,12 +133,11 @@
         copy.start()
 
     barrier = pltpu.get_barrier_semaphore()
-    for step in (4, 12, 3, 13, 2, 14, 1, 15):
+    for step in (2, 14, 1, 15):
         pl.semaphore_signal(barrier, inc=1, device_id=(r, (z + step) % cols_n), device_id_type=MESH)
-
-    @pl.loop(1, rows_n)
-    def _(step):
-        pl.semaphore_signal(barrier, inc=1, device_id=((r + step) % rows_n, z), device_id_type=MESH)
+    for offset in diagonal + near:
+        pl.semaphore_signal(barrier, inc=1, device_id=(device_at(offset, False), z), device_id_type=MESH)
+    pl.semaphore_signal(barrier, inc=1, device_id=(sibling, z), device_id_type=MESH)
 
     for copy in loads:
         copy.wait()
@@ -160,21 +147,18 @@
     col_total[...] = jnp.zeros_like(col_total)
     own_total[...] = jnp.zeros_like(own_total)
 
-    pl.semaphore_wait(barrier, 8 + rows_n - 1)
-
-    def row_copy(src, dst, step):
-        return pltpu.make_async_remote_copy(
-            src_ref=row_in.at[src],
-            dst_ref=row_in.at[dst],
-            send_sem=row_send.at[dst],
-            recv_sem=row_recv.at[dst],
+    pl.semaphore_wait(barrier, 13)
+
+    def row_copy(src, dst, half, step):
+        place = pl.ds(half * half_rows, half_rows)
+        return pltpu.make_async_remote_copy(
+            src_ref=row_in.at[src, place],
+            dst_ref=row_in.at[dst, place],
+            send_sem=row_send.at[dst, half],
+            recv_sem=row_recv.at[dst, half],
             device_id=(r, (z + cols_n + step) % cols_n),
             device_id_type=MESH,
         )
-
-    def device_at(offset, other):
-        target = (((x + offset[0]) % side) * side + (y + offset[1]) % side) * 2
-        return target + (1 - core if other else core)
 
     def col_copy(offset, step):
         dst = slot_of((offset[0] + step[0], offset[1] + step[1]))
@@ -219,8 +203,9 @@
             device_id_type=MESH,
         )
 
-    row_copy(0, 1, 1).start()
-    row_copy(0, 2, -2).start()
+    for half in range(2):
+        row_copy(0, 1, half, 1).start()
+        row_copy(0, 2, half, -2).start()
     sib_copy(0).start()
     for offset in near + diagonal:
         col_copy((0, 0), offset).start()
@@ -270,48 +255,10 @@
         for o in range(4 * c, 4 * c + 4):
             make_stream(1, o)
 
-    def take_row(k):
-        row_copy(0, k, 0).wait_recv()
+    def take_row(k, half):
+        row_copy(0, k, half, 0).wait_recv()
         if k + 2 < held:
-            row_copy(k, k + 2, 2 if k % 2 else -2).start()
-
-    def event_0():
-        take_row(1)
-        take_columns(near)
-        take_row(2)
-        make_weights(0)
-        use_columns(0)
-
-    def event_1():
-        take_columns(diagonal)
-        take_row(3)
-        use_columns(1)
-
-    def event_2():
-        take_row(4)
-        make_weights(1)
-
-    def event_4():
-        own_units(0)
-        take_columns(far)
-        take_row(5)
-        use_columns(2)
-
-    def event_5():
-        use_columns(3)
-
-    def event_6():
-        take_row(6)
-
-    def event_8():
-        make_weights(2)
-
-    def event_12():
-        take_row(7)
-        take_row(8)
-        make_weights(3)
-
-    events = {1: event_1, 2: event_2, 4: event_4, 5: event_5, 6: event_6, 8: event_8, 12: event_12}
+            row_copy(k, k + 2, half, 2 if k % 2 else -2).start()
 
     def send_rows(p):
         both = row_total[p]
@@ -329,36 +276,12 @@
                 if (b, o) != (0, 0):
                     col_part_copy(b, o).start()
 
-    def finish_15():
-        send_rows(3)
-        send_columns(3)
-
-    finishes = {
-        5: lambda: send_rows(1),
-        7: lambda: send_rows(0),
-        11: lambda: send_rows(2),
-        12: lambda: send_columns(0),
-        13: lambda: send_columns(1),
-        14: lambda: send_columns(2),
-        15: finish_15,
-    }
-
-    def unit(u):
-        return lookup([p for p, _ in units], u), lookup([c for _, c in units], u)
-
-    def run(table, u, parity):
-        for when, event in table.items():
-            if when % 2 == parity:
-                pl.when(u == when)(event)
-
-    def products(u, tile):
-        p, c = unit(u)
-        place = pl.ds(pl.multiple_of(c * chunk, chunk), chunk)
+    def products(p, c, tile):
+        place = pl.ds(c * chunk, chunk)
         tile[...] = dot(stream[place, :], weights[p])
 
-    def apply(u, tile):
-        p, c = unit(u)
-        place = pl.ds(pl.multiple_of(c * chunk, chunk), chunk)
+    def apply(p, c, tile):
+        place = pl.ds(c * chunk, chunk)
         sq = col_sq[place, :]
         exponent = tile[...] - jnp.concatenate([sq, sq], axis=1) - row_sq[p, 0:1, :]
         high, low = split(jnp.exp2(exponent))
@@ -376,28 +299,81 @@
         high, low = split(jnp.exp2(tile[...] - col_sq[place, :] - own_sq[0:1, :]))
         own_total[...] += dot(dirs[:, place], high) + dot(dirs[:, place], low)
 
-    def own_units(c):
-        own_products(c, own_a)
-        own_products(c + 1, own_b)
-        own_apply(c, own_a)
-        own_apply(c + 1, own_b)
-
-    event_0()
-    products(0, tile_a)
-
-    @pl.loop(0, len(units) // 2)
-    def _(w):
-        u = 2 * w
-        run(events, u + 1, 1)
-        products(u + 1, tile_b)
-        apply(u, tile_a)
-        run(finishes, u, 0)
-        run(events, u + 2, 0)
-        products(jnp.minimum(u + 2, len(units) - 1), tile_a)
-        apply(u + 1, tile_b)
-        run(finishes, u + 1, 1)
-
-    own_units(2)
+    waiting = []
+
+    def flush():
+        while waiting:
+            waiting.pop()()
+
+    def unit(p, c, tile):
+        products(p, c, tile)
+        flush()
+        waiting.append(lambda: apply(p, c, tile))
+
+    def own(c, tile):
+        own_products(c, tile)
+        flush()
+        waiting.append(lambda: own_apply(c, tile))
+
+    take_row(1, 0)
+    take_row(1, 1)
+    take_row(2, 0)
+    take_columns(near)
+    take_row(2, 1)
+    make_weights(0)
+    use_columns(0)
+    unit(0, 0, tile_a)
+    own(0, own_a)
+    flush()
+    take_row(3, 0)
+    take_columns(diagonal)
+    take_row(4, 0)
+    take_row(3, 1)
+    use_columns(1)
+    unit(0, 1, tile_b)
+    flush()
+    take_row(4, 1)
+    make_weights(1)
+    unit(1, 0, tile_a)
+    own(1, own_b)
+    unit(1, 1, tile_b)
+    flush()
+    take_row(5, 0)
+    take_columns(far)
+    take_row(6, 0)
+    take_row(5, 1)
+    use_columns(2)
+    unit(0, 2, tile_a)
+    take_row(6, 1)
+    make_weights(2)
+    unit(1, 2, tile_b)
+    use_columns(3)
+    unit(0, 3, tile_a)
+    unit(1, 3, tile_b)
+    send_rows(0)
+    unit(2, 2, tile_a)
+    send_rows(1)
+    unit(2, 3, tile_b)
+    flush()
+    for half in range(2):
+        take_row(7, half)
+        take_row(8, half)
+    make_weights(3)
+    unit(3, 3, tile_a)
+    unit(3, 2, tile_b)
+    send_columns(3)
+    unit(3, 1, tile_a)
+    send_columns(2)
+    unit(3, 0, tile_b)
+    unit(2, 1, tile_a)
+    send_rows(3)
+    unit(2, 0, tile_b)
+    send_columns(1)
+    own(2, own_a)
+    send_rows(2)
+    send_columns(0)
+    own(3, own_b)
+    flush()
 
     direction = row_in[0, block : block + rhs, :]
     residual = res_ref[...]
@@ -428,25 +404,28 @@
             device_id_type=MESH,
         )
 
-    def r_copy(step):
+    def r_copy(b, o):
+        dx, dy = offsets[o]
+        dst = 2 * slot_of((-dx, -dy)) + b
         return pltpu.make_async_remote_copy(
             src_ref=stat_r.at[0],
-            dst_ref=stat_r.at[step],
-            send_sem=sr_send.at[step],
-            recv_sem=sr_recv.at[step],
-            device_id=((r + step) % rows_n, z),
-            device_id_type=MESH,
-        )
-
+            dst_ref=stat_r.at[dst],
+            send_sem=sr_send.at[2 * o + b],
+            recv_sem=sr_recv.at[dst],
+            device_id=(device_at((dx, dy), b == 1), z),
+            device_id_type=MESH,
+        )
+
+    others = [(b, o) for o in range(plane - 1, -1, -1) for b in range(2) if (b, o) != (0, 0)]
     for step in sorted(range(1, cols_n), key=lambda step: -min(step, cols_n - step)):
         z_copy(step).start()
     for step in range(1, cols_n):
         z_copy(step).wait_recv()
     stat_r[0] = jnp.sum(stat_z[...], axis=0)
-    for step in range(1, rows_n):
-        r_copy(step).start()
-    for step in range(1, rows_n):
-        r_copy(step).wait_recv()
+    for b, o in others:
+        r_copy(b, o).start()
+    for b, o in others:
+        r_copy(b, o).wait_recv()
     sums = jnp.broadcast_to(jnp.sum(stat_r[...], axis=0), (rhs, block))
 
     def take(q):
@@ -456,18 +435,18 @@
     step_size = norm_now / curvature
     norm_next = jnp.maximum(norm_now - step_size * (2.0 * cross - step_size * square), 0.0)
     ratio = norm_next / norm_now
-    next_residual = residual - step_size * applied
-    nsol_ref[...] = sol_ref[...] + step_size * direction
-    nres_ref[...] = next_residual
-    ndir_ref[...] = next_residual + ratio * direction
+    applied_ref[...] = applied
+    step_ref[...] = jnp.broadcast_to(step_size, (rhs, block))
+    ratio_ref[...] = jnp.broadcast_to(ratio, (rhs, block))
 
     for k in range(1, held):
-        row_copy(0, k, 0).wait_send()
+        for half in range(2):
+            row_copy(0, k, half, 0).wait_send()
         part_copy(k).wait_send()
     for step in range(1, cols_n):
         z_copy(step).wait_send()
-    for step in range(1, rows_n):
-        r_copy(step).wait_send()
+    for b, o in others:
+        r_copy(b, o).wait_send()
     for o in range(plane):
         sib_copy(o).wait_send()
         if o > 0:
@@ -482,10 +461,10 @@
     dma = pltpu.SemaphoreType.DMA
     out = jax.ShapeDtypeStruct((rhs, block), f32)
     span = rows_n * block
-    return pl.pallas_call(
+    applied, step_size, ratio = pl.pallas_call(
         kernel,
         out_shape=(out, out, out),
-        in_specs=[pl.BlockSpec(memory_space=pltpu.HBM)] * 4,
+        in_specs=[pl.BlockSpec(memory_space=pltpu.HBM)] * 3,
         out_specs=(vmem, vmem, vmem),
         scratch_shapes=[
             pltpu.VMEM((2, plane, block + rhs, block), f32),
@@ -512,14 +491,13 @@
             pltpu.VMEM((cols_n, 1, block), f32),
             pltpu.VMEM((rows_n, 1, block), f32),
             pltpu.VMEM((rhs, block), f32),
-            pltpu.VMEM((rhs, block), f32),
-            dma((4,)),
+            dma((3,)),
             dma((plane,)),
             dma((plane,)),
             dma((plane,)),
             dma((plane,)),
-            dma((held,)),
-            dma((held,)),
+            dma((held, 2)),
+            dma((held, 2)),
             dma((held,)),
             dma((held,)),
             dma((2, plane)),
@@ -533,7 +511,9 @@
             collective_id=0, has_side_effects=True, vmem_limit_bytes=60 * 1024 * 1024
         ),
         name="cg_step",
-    )(points, solution, residual, direction)
+    )(points, residual, direction)
+    next_residual = residual - step_size * applied
+    return solution + step_size * direction, next_residual, next_residual + ratio * direction
 
 
 def solution(mesh):

time: 68.4 us -> 64.7 us (0.946)
  local copies, waits for them, and re-layouts: 2.6 us -> 0.01 us
  Pallas kernels: 64.9 us -> 62.5 us
  other arithmetic: 0 us -> 1.34 us
    unnamed x7 -> x6, local copies, waits for them, and re-layouts: 2.6 us -> 0.01 us
    pallas_call x1, Pallas kernels: 64.9 us -> 62.5 us  [per_device(): pl.pallas_call(kernel, out_shape=(out, out, out), in_specs=[pl.BlockSpec(...]
    add x0 -> x1, other arithmetic: none -> 1.34 us  [per_device(): next_residual + ratio * direction]
where the time goes in v5:
time: 64.7 us; the launch traced here: 64.5 us
  Pallas kernels  62.5 us (97%)
  other arithmetic  1.34 us (2%)
  between operations  0.69 us (1%)
    pallas_call x1, Pallas kernels, per_device(): pl.pallas_call(kernel, out_shape=(out, out, out), in_specs=[pl.BlockSpec(...  62.5 us
    add x1, other arithmetic, per_device(): next_residual + ratio * direction  1.34 us

profile of v5, /device:TPU:1, one launch (start us, length us, event | category | flops | bytes accessed | tf_op | source)
XLA Modules:
  0.0 64.5 jit_solution(2173290374233992801)
XLA Ops:
  0.6 0.0 copy-start
  0.6 0.0 copy-start.1
  0.7 0.0 copy-start.2
  0.7 62.5 %cg_step.1 = (f32[16,128]{1,0:T(8,128)}, f32[16,128]{1,0:T(8,128)}, f32[16,128]{1,0:T(8,128)}) custom-call(f32[128,128]{1,0:T(8,128)} %pts_hbm.1, f32[16,128]{1,0:T(8,128)} %res_hbm.1, f32[16,128]{1,0:T(8,128)} %dir_hbm.1), custom_call_target="tpu_custom_call" | custom-call | tf_op jit(solution)/shard_map/cg_step/pallas_call | solution.py:464
  63.1 0.0 copy-done
  63.1 0.0 copy-done.1
  63.2 0.0 copy-done.2
  63.2 1.3 %multiply_add_fusion = (f32[16,128]{1,0:T(8,128)}, f32[16,128]{1,0:T(8,128)}, f32[16,128]{1,0:T(8,128)}) fusion(f32[16,128]{1,0:T(8,128)} %get-tuple-element.8, f32[16,128]{1,0:T(8,128)S(1)} %copy-done.1, f32[16,128]{1,0:T(8,128)S(1)} %copy-done, f32[16,128]{1,0:T(8,128)} %get-tuple-element.6, f32[16,128]{1,0:T(8,128)} %get-tuple-element.7, ...), kind=kLoop, calls=%fused_computation | loop fusion | flops 12288 | bytes 73728 | tf_op jit(solution)/shard_map/add | solution.py:516
Async XLA Ops:
  0.6 62.5 %copy-start = (f32[16,128]{1,0:T(8,128)S(1)}, f32[16,128]{1,0:T(8,128)}, u32[]{:S(2)}) copy-start(f32[16,128]{1,0:T(8,128)} %res_hbm.1) | copy-start | bytes 24580
  0.6 62.5 %copy-start.1 = (f32[16,128]{1,0:T(8,128)S(1)}, f32[16,128]{1,0:T(8,128)}, u32[]{:S(2)}) copy-start(f32[16,128]{1,0:T(8,128)} %dir_hbm.1) | copy-start | bytes 24580
  0.7 62.5 %copy-start.2 = (f32[16,128]{1,0:T(8,128)S(1)}, f32[16,128]{1,0:T(8,128)}, u32[]{:S(2)}) copy-start(f32[16,128]{1,0:T(8,128)} %param.5) | copy-start | bytes 24580

commit v6 on v5

--- a/solution.py
+++ b/solution.py
@@ -84,6 +84,7 @@
     tile_b,
     own_a,
     own_b,
+    kept,
     row_total,
     col_total,
     own_total,
@@ -266,13 +267,16 @@
         for half in range(2):
             k = 2 * p + 1 + half
             part[k] = both[:, half * block : (half + 1) * block]
-            part_copy(k).start()
+        for half in range(2):
+            part_copy(2 * p + 1 + half).start()
 
     def send_columns(c):
         for o in range(4 * c, 4 * c + 4):
             for b in range(2):
                 place = slice((2 * o + b) * block, (2 * o + b + 1) * block)
                 col_part[b, o] = col_total[0:rhs, place] + col_total[rhs : 2 * rhs, place]
+        for o in range(4 * c + 3, 4 * c - 1, -1):
+            for b in range(2):
                 if (b, o) != (0, 0):
                     col_part_copy(b, o).start()
 
@@ -288,6 +292,18 @@
         row_total[p] += dot(dirs[:, place], high) + dot(dirs[:, place], low)
         col_total[:, place] += dot_turned(row_dirs[p], high) + dot_turned(row_dirs[p], low)
 
+    def late_apply(c, tile):
+        place = pl.ds(c * chunk, chunk)
+        sq = col_sq[place, :]
+        exponent = tile[...] - jnp.concatenate([sq, sq], axis=1) - row_sq[3, 0:1, :]
+        high, low = split(jnp.exp2(exponent))
+        kept[0, c], kept[1, c] = high, low
+        row_total[3] += dot(dirs[:, place], high) + dot(dirs[:, place], low)
+
+    def late_columns(c):
+        place = pl.ds(c * chunk, chunk)
+        col_total[:, place] += dot_turned(row_dirs[3], kept[0, c]) + dot_turned(row_dirs[3], kept[1, c])
+
     own_weights[...], own_sq[...] = turn(row_in[0, 0:block, :])
 
     def own_products(c, tile):
@@ -309,6 +325,11 @@
         products(p, c, tile)
         flush()
         waiting.append(lambda: apply(p, c, tile))
+
+    def late_unit(c, tile):
+        products(3, c, tile)
+        flush()
+        waiting.append(lambda: late_apply(c, tile))
 
     def own(c, tile):
         own_products(c, tile)
@@ -333,44 +354,48 @@
     unit(0, 1, tile_b)
     flush()
     take_row(4, 1)
+    take_columns(far[:2])
     make_weights(1)
     unit(1, 0, tile_a)
     own(1, own_b)
-    unit(1, 1, tile_b)
     flush()
     take_row(5, 0)
-    take_columns(far)
+    take_columns(far[2:3])
+    use_columns(2)
+    unit(0, 2, tile_b)
     take_row(6, 0)
     take_row(5, 1)
-    use_columns(2)
-    unit(0, 2, tile_a)
+    take_columns(far[3:])
+    unit(1, 2, tile_a)
     take_row(6, 1)
     make_weights(2)
-    unit(1, 2, tile_b)
     use_columns(3)
-    unit(0, 3, tile_a)
-    unit(1, 3, tile_b)
+    unit(2, 2, tile_b)
+    unit(2, 0, tile_a)
+    unit(2, 3, tile_b)
+    unit(2, 1, tile_a)
+    unit(0, 3, tile_b)
+    send_rows(2)
+    flush()
     send_rows(0)
-    unit(2, 2, tile_a)
-    send_rows(1)
-    unit(2, 3, tile_b)
-    flush()
     for half in range(2):
         take_row(7, half)
         take_row(8, half)
     make_weights(3)
-    unit(3, 3, tile_a)
-    unit(3, 2, tile_b)
+    for c, tile in ((0, tile_a), (1, tile_b), (2, tile_a), (3, tile_b)):
+        late_unit(c, tile)
+    unit(1, 3, tile_a)
+    send_rows(3)
+    unit(1, 1, tile_b)
+    late_columns(3)
     send_columns(3)
-    unit(3, 1, tile_a)
+    late_columns(2)
     send_columns(2)
-    unit(3, 0, tile_b)
-    unit(2, 1, tile_a)
-    send_rows(3)
-    unit(2, 0, tile_b)
+    own(2, own_a)
+    send_rows(1)
+    late_columns(1)
     send_columns(1)
-    own(2, own_a)
-    send_rows(2)
+    late_columns(0)
     send_columns(0)
     own(3, own_b)
     flush()
@@ -378,14 +403,18 @@
     direction = row_in[0, block : block + rhs, :]
     residual = res_ref[...]
     applied = own_total[0:rhs] + own_total[rhs : 2 * rhs] + col_part[0, 0] + noise_var * direction
-    for k in range(8, 0, -1):
-        part_copy(k).wait_recv()
-        applied = applied + part_in[k]
     for o in range(plane):
         for b in range(2):
             if (b, o) != (0, 0):
                 col_part_copy(b, o).wait_recv()
-                applied = applied + col_part_in[b, slot_of((-offsets[o][0], -offsets[o][1]))]
+    for b in range(2):
+        for o in range(plane):
+            if (b, o) != (0, 0):
+                applied = applied + col_part_in[b, o]
+    for k in range(1, held):
+        part_copy(k).wait_recv()
+    for k in range(1, held):
+        applied = applied + part_in[k]
 
     lane = lax.broadcasted_iota(jnp.int32, (rhs, block), 1)
     line = lax.broadcasted_iota(jnp.int32, (rhs, block), 0)
@@ -481,6 +510,7 @@
             pltpu.VMEM((chunk, 2 * block), f32),
             pltpu.VMEM((chunk, block), f32),
             pltpu.VMEM((chunk, block), f32),
+            pltpu.VMEM((2, chunks, chunk, 2 * block), bf16),
             pltpu.VMEM((pairs, 2 * rhs, 2 * block), f32),
             pltpu.VMEM((2 * rhs, span), f32),
             pltpu.VMEM((2 * rhs, block), f32),

time: 64.7 us -> 64 us (0.989)
  Pallas kernels: 62.5 us -> 61.7 us
    pallas_call x1, Pallas kernels: 62.5 us -> 61.7 us  [per_device(): pl.pallas_call(kernel, out_shape=(out, out, out), in_specs=[pl.BlockSpec(...]
where the time goes in v6:
time: 64 us; the launch traced here: 63.8 us
  Pallas kernels  61.7 us (96%)
  other arithmetic  1.34 us (2%)
  between operations  0.69 us (1%)
    pallas_call x1, Pallas kernels, per_device(): pl.pallas_call(kernel, out_shape=(out, out, out), in_specs=[pl.BlockSpec(...  61.7 us
    add x1, other arithmetic, per_device(): next_residual + ratio * direction  1.34 us

profile of v6, /device:TPU:1, one launch (start us, length us, event | category | flops | bytes accessed | tf_op | source)
XLA Modules:
  0.0 63.8 jit_solution(4389977645148855184)
XLA Ops:
  0.6 0.0 copy-start
  0.6 0.0 copy-start.1
  0.7 0.0 copy-start.2
  0.7 61.7 %cg_step.1 = (f32[16,128]{1,0:T(8,128)}, f32[16,128]{1,0:T(8,128)}, f32[16,128]{1,0:T(8,128)}) custom-call(f32[128,128]{1,0:T(8,128)} %pts_hbm.1, f32[16,128]{1,0:T(8,128)} %res_hbm.1, f32[16,128]{1,0:T(8,128)} %dir_hbm.1), custom_call_target="tpu_custom_call" | custom-call | tf_op jit(solution)/shard_map/cg_step/pallas_call | solution.py:493
  62.4 0.0 copy-done
  62.4 0.0 copy-done.1
  62.4 0.0 copy-done.2
  62.4 1.3 %multiply_add_fusion = (f32[16,128]{1,0:T(8,128)}, f32[16,128]{1,0:T(8,128)}, f32[16,128]{1,0:T(8,128)}) fusion(f32[16,128]{1,0:T(8,128)} %get-tuple-element.8, f32[16,128]{1,0:T(8,128)S(1)} %copy-done.1, f32[16,128]{1,0:T(8,128)S(1)} %copy-done, f32[16,128]{1,0:T(8,128)} %get-tuple-element.6, f32[16,128]{1,0:T(8,128)} %get-tuple-element.7, ...), kind=kLoop, calls=%fused_computation | loop fusion | flops 12288 | bytes 73728 | tf_op jit(solution)/shard_map/add | solution.py:546
Async XLA Ops:
  0.6 61.8 %copy-start = (f32[16,128]{1,0:T(8,128)S(1)}, f32[16,128]{1,0:T(8,128)}, u32[]{:S(2)}) copy-start(f32[16,128]{1,0:T(8,128)} %res_hbm.1) | copy-start | bytes 24580
  0.6 61.8 %copy-start.1 = (f32[16,128]{1,0:T(8,128)S(1)}, f32[16,128]{1,0:T(8,128)}, u32[]{:S(2)}) copy-start(f32[16,128]{1,0:T(8,128)} %dir_hbm.1) | copy-start | bytes 24580
  0.7 61.8 %copy-start.2 = (f32[16,128]{1,0:T(8,128)S(1)}, f32[16,128]{1,0:T(8,128)}, u32[]{:S(2)}) copy-start(f32[16,128]{1,0:T(8,128)} %param.5) | copy-start | bytes 24580

commit v7 on v6

--- a/solution.py
+++ b/solution.py
@@ -384,8 +384,9 @@
     make_weights(3)
     for c, tile in ((0, tile_a), (1, tile_b), (2, tile_a), (3, tile_b)):
         late_unit(c, tile)
+    flush()
+    send_rows(3)
     unit(1, 3, tile_a)
-    send_rows(3)
     unit(1, 1, tile_b)
     late_columns(3)
     send_columns(3)
@@ -448,11 +449,26 @@
     others = [(b, o) for o in range(plane - 1, -1, -1) for b in range(2) if (b, o) != (0, 0)]
     for step in sorted(range(1, cols_n), key=lambda step: -min(step, cols_n - step)):
         z_copy(step).start()
+    for k in range(1, held):
+        for half in range(2):
+            row_copy(0, k, half, 0).wait_send()
+        part_copy(k).wait_send()
+    for o in range(plane):
+        sib_copy(o).wait_send()
+        if o > 0:
+            col_copy((0, 0), offsets[o]).wait_send()
+        for b in range(2):
+            if (b, o) != (0, 0):
+                col_part_copy(b, o).wait_send()
     for step in range(1, cols_n):
         z_copy(step).wait_recv()
     stat_r[0] = jnp.sum(stat_z[...], axis=0)
     for b, o in others:
         r_copy(b, o).start()
+    for step in range(1, cols_n):
+        z_copy(step).wait_send()
+    for b, o in others:
+        r_copy(b, o).wait_send()
     for b, o in others:
         r_copy(b, o).wait_recv()
     sums = jnp.broadcast_to(jnp.sum(stat_r[...], axis=0), (rhs, block))
@@ -467,22 +483,6 @@
     applied_ref[...] = applied
     step_ref[...] = jnp.broadcast_to(step_size, (rhs, block))
     ratio_ref[...] = jnp.broadcast_to(ratio, (rhs, block))
-
-    for k in range(1, held):
-        for half in range(2):
-            row_copy(0, k, half, 0).wait_send()
-        part_copy(k).wait_send()
-    for step in range(1, cols_n):
-        z_copy(step).wait_send()
-    for b, o in others:
-        r_copy(b, o).wait_send()
-    for o in range(plane):
-        sib_copy(o).wait_send()
-        if o > 0:
-            col_copy((0, 0), offsets[o]).wait_send()
-        for b in range(2):
-            if (b, o) != (0, 0):
-                col_part_copy(b, o).wait_send()
 
 
 def per_device(points, solution, residual, direction):

time: 64 us -> 64.2 us (level)
  no operation moved by 1% of the time
where the time goes in v7:
time: 64.2 us; the launch traced here: 63.9 us
  Pallas kernels  61.9 us (96%)
  other arithmetic  1.34 us (2%)
  between operations  0.69 us (1%)
    pallas_call x1, Pallas kernels, per_device(): pl.pallas_call(kernel, out_shape=(out, out, out), in_specs=[pl.BlockSpec(...  61.9 us
    add x1, other arithmetic, per_device(): next_residual + ratio * direction  1.34 us

profile of v7, /device:TPU:1, one launch (start us, length us, event | category | flops | bytes accessed | tf_op | source)
XLA Modules:
  0.0 63.9 jit_solution(16177575971240338101)
XLA Ops:
  0.6 0.0 copy-start
  0.6 0.0 copy-start.1
  0.7 0.0 copy-start.2
  0.7 61.9 %cg_step.1 = (f32[16,128]{1,0:T(8,128)}, f32[16,128]{1,0:T(8,128)}, f32[16,128]{1,0:T(8,128)}) custom-call(f32[128,128]{1,0:T(8,128)} %pts_hbm.1, f32[16,128]{1,0:T(8,128)} %res_hbm.1, f32[16,128]{1,0:T(8,128)} %dir_hbm.1), custom_call_target="tpu_custom_call" | custom-call | tf_op jit(solution)/shard_map/cg_step/pallas_call | solution.py:493
  62.6 0.0 copy-done
  62.6 0.0 copy-done.1
  62.6 0.0 copy-done.2
  62.6 1.3 %multiply_add_fusion = (f32[16,128]{1,0:T(8,128)}, f32[16,128]{1,0:T(8,128)}, f32[16,128]{1,0:T(8,128)}) fusion(f32[16,128]{1,0:T(8,128)} %get-tuple-element.8, f32[16,128]{1,0:T(8,128)S(1)} %copy-done.1, f32[16,128]{1,0:T(8,128)S(1)} %copy-done, f32[16,128]{1,0:T(8,128)} %get-tuple-element.6, f32[16,128]{1,0:T(8,128)} %get-tuple-element.7, ...), kind=kLoop, calls=%fused_computation | loop fusion | flops 12288 | bytes 73728 | tf_op jit(solution)/shard_map/add | solution.py:546
Async XLA Ops:
  0.6 61.9 %copy-start = (f32[16,128]{1,0:T(8,128)S(1)}, f32[16,128]{1,0:T(8,128)}, u32[]{:S(2)}) copy-start(f32[16,128]{1,0:T(8,128)} %res_hbm.1) | copy-start | bytes 24580
  0.6 61.9 %copy-start.1 = (f32[16,128]{1,0:T(8,128)S(1)}, f32[16,128]{1,0:T(8,128)}, u32[]{:S(2)}) copy-start(f32[16,128]{1,0:T(8,128)} %dir_hbm.1) | copy-start | bytes 24580
  0.7 61.9 %copy-start.2 = (f32[16,128]{1,0:T(8,128)S(1)}, f32[16,128]{1,0:T(8,128)}, u32[]{:S(2)}) copy-start(f32[16,128]{1,0:T(8,128)} %param.5) | copy-start | bytes 24580
